TPU v7x, 32 devices: a whole 2x2x4 slice. The times are simulated.
32 devices in a mesh: lat: 4 (over y, x), grp: 8 (over z, core).
Axes of the slice: x: 2, y: 2, z: 4, core: 2. Of those that a mesh axis runs over, the one named last changes fastest.
Arguments:
- fields: float32 [256, 30, 64, 128], P('grp', None, 'lat'), may hold values from -6 to 6
- diffusion: float32 [64, 128], P('lat'), may hold values from 0.12 to 0.245
- mixing: float32 [30, 30], replicated, may hold values from -0.08 to 1
- heating: float32 [30, 64, 128], P(None, 'lat'), may hold values from -2 to 2
- land_mask: int32 [64, 128], P('lat'), may hold values 0 or 1
- conv_weight: float32 [32, 27], replicated, may hold values from -1.25 to 1.25
- head_weight: float32 [32, 64, 128], P(None, 'lat'), may hold values from -0.01171875 to 0.01171875
- counts: int32 [256], replicated, may hold values from 0 to 32, as said below
- source: int32 [256], replicated, may hold values from 0 to 255, as said below
Outputs:
- new_fields: float32 [256, 30, 64, 128], P('grp', None, 'lat')
- scores: float32 [256], P('grp')
- slot_weight: float32 [256], P('grp')
Inputs may be any that keep to these rules, and one draw needn't show every extreme that they name: Members 32 g to 32 g + 31 form group g. In every group exactly one member has a count of 2 or more and every group has a member of count 0; the counts sum to 256. source[s] = s where the member s has a count of 1 or more. Every slot s of count 0 takes the member of count 2 or more of one other group, the same group for all such slots of s's group, each group's such member is taken by the slots of exactly one other group, and a member of count c is taken by c - 1 slots.
All inputs are finite; a program needn't handle non-finite values. No bound on the sum of `land_mask` on one device may be relied on, other than what follows from the above.
Results may differ from a plain program's by a relative error of at most 0.0003.
Values sent between devices are 32-bit elements; how exact they have to be, the bound alone decides.
A program may use at most 128 MiB of HBM per device.

v0:
```python
import jax
import jax.numpy as jnp
from jax import lax
from jax.sharding import PartitionSpec as P

LEV = 10
STEPS = 4


def with_halo(value, sides, width):
    for axis, dim in sides:
        size, length = (lax.axis_size(axis), value.shape[dim])
        up = [(i, (i + 1) % size) for i in range(size - 1)]
        down = [(j, i) for i, j in up]
        last = lax.slice_in_dim(value, length - width, length, axis=dim)
        initial = lax.slice_in_dim(value, 0, width, axis=dim)
        before = lax.ppermute(last, axis, up)
        after = lax.ppermute(initial, axis, down)
        value = jnp.concatenate([before, value, after], axis=dim)
    return value


def advance(values, diffusion, mixing, heating):
    padded = with_halo(values, (("lat", 2),), 1)
    laplace = (
        padded[:, :, 2:]
        + padded[:, :, :-2]
        + jnp.roll(values, 1, 3)
        + jnp.roll(values, -1, 3)
        - 4.0 * values
    )
    smooth = values + diffusion * laplace
    mixed = jnp.einsum("ij,mjac->miac", mixing, smooth, precision=lax.Precision.HIGHEST)
    return mixed + heating - 0.05 * mixed * mixed * mixed


def run_steps(values, diffusion, mixing, heating):
    for repeat in range(STEPS):
        values = advance(values, diffusion, mixing, heating)
    return values


def score_terms(padded, conv_weight, head_weight):
    height = padded.shape[2] - 2
    members_here = padded.shape[0]
    taps = [
        jnp.roll(padded[:, :, shift_lat : shift_lat + height], -shift_lon, 3)
        for shift_lat in range(3)
        for shift_lon in (-1, 0, 1)
    ]
    patches = jnp.stack(taps, 2).reshape(members_here, 27, height * padded.shape[3])
    hidden = jax.nn.relu(
        jnp.einsum("ck,mkp->mcp", conv_weight, patches, precision=lax.Precision.HIGHEST)
    )
    return jnp.einsum(
        "mcp,cp->m",
        hidden,
        head_weight.reshape(head_weight.shape[0], -1),
        precision=lax.Precision.HIGHEST,
    )


def local(fields, diffusion, mixing, heating, land_mask, conv_weight, head_weight, counts, source):
    members_here = fields.shape[0]
    total_members = counts.shape[0]
    offset = lax.axis_index("grp") * members_here
    local_counts = lax.dynamic_slice_in_dim(counts, offset, members_here)
    local_source = lax.dynamic_slice_in_dim(source, offset, members_here)
    hot_flag = (local_counts >= 2).astype(jnp.float32)
    killed = local_source != offset + jnp.arange(members_here, dtype=jnp.int32)
    donor_group = jnp.max(jnp.where(killed, local_source // members_here, 0))
    final = run_steps(fields, diffusion, mixing, heating)
    hot_member = jnp.sum(final * hot_flag[:, None, None, None], 0)
    gathered = lax.all_gather(hot_member[None], "grp", axis=0, tiled=True)
    donor_final = lax.dynamic_index_in_dim(gathered, donor_group, 0, keepdims=False)
    new_fields = jnp.where(killed[:, None, None, None], donor_final[None], final)
    land_float = land_mask.astype(jnp.float32)
    temper = final[:, 0]
    moisture = final[:, LEV]
    inputs = jnp.stack([temper * land_float, moisture, temper * (1.0 - land_float)], 1)
    padded = with_halo(inputs, (("lat", 2),), 1)
    partial_terms = score_terms(padded, conv_weight, head_weight)
    scores = lax.psum(partial_terms, "lat")
    all_scores = lax.all_gather(scores, "grp", axis=0, tiled=True)
    weights = jnp.exp(all_scores)
    weights = weights / jnp.mean(weights)
    selector = (
        local_source[:, None] == jnp.arange(total_members, dtype=jnp.int32)[None, :]
    ).astype(jnp.float32)
    chosen_weight = jnp.sum(selector * weights[None, :], 1)
    chosen_count = jnp.sum(selector * counts.astype(jnp.float32)[None, :], 1)
    slot_weight = chosen_weight / chosen_count
    return (new_fields, scores, slot_weight)


def solution(mesh):
    return jax.shard_map(
        local,
        mesh=mesh,
        in_specs=(
            P("grp", None, "lat", None),
            P("lat", None),
            P(),
            P(None, "lat", None),
            P("lat", None),
            P(),
            P(None, "lat", None),
            P(),
            P(),
        ),
        out_specs=(P("grp", None, "lat", None), P("grp"), P("grp")),
        check_vma=False,
    )
```

profile of v0, /device:TPU:0, one launch (start us, length us, event | category | flops | bytes accessed | tf_op | source)
XLA Modules:
  0.0 371.1 jit_solution(6812917586705588738)
XLA Ops:
  7.2 6.5 %copy.77 = f32[32,30,16,128]{3,1,2,0:T(8,128)S(1)} copy(f32[32,30,16,128]{3,2,1,0:T(8,128)} %param.9) | data formatting | bytes 15728640 | tf_op args[0]
  15.1 5.7 %collective-permute-start.1 = (f32[32,30,1,128]{3,1,2,0:T(8,128)S(1)}, f32[32,30,1,128]{3,1,2,0:T(8,128)S(1)}, u32[]{:S(2)}, u32[]{:S(2)}) collective-permute-start(f32[32,30,1,128]{3,1,2,0:T(8,128)S(1)} %get-tuple-element.48), channel_id=1, source_target_pairs={{0,8},{8,16},{16,24},{1,9},{9,17},{17,25},{2,10},{10,18},{18,26},{... | collective-permute-start | bytes 1474568 | tf_op jit(solution)/shard_map/ppermute | solution.py:17
  20.8 7.3 %fusion.123 = (f32[32,30,16,127]{3,1,2,0:T(8,128)}, f32[32,30,16,127]{3,1,2,0:T(8,128)}) fusion(f32[32,30,16,128]{3,1,2,0:T(8,128)S(1)} %copy.77), kind=kLoop, calls=%fused_computation.156 | loop fusion | bytes 31211520 | tf_op jit(solution)/shard_map/jit(_roll_static)/slice | solution.py:29
  28.1 7.3 %fusion.124 = (f32[32,30,16,1]{3,1,2,0:T(8,128)}, f32[32,30,16,1]{3,1,2,0:T(8,128)}) fusion(f32[32,30,16,128]{3,1,2,0:T(8,128)S(1)} %copy.77), kind=kLoop, calls=%fused_computation.157 | loop fusion | bytes 245760 | tf_op jit(solution)/shard_map/jit(_roll_static)/slice | solution.py:29
  39.6 26.9 %fusion = f32[32,30,16,128]{3,1,2,0:T(8,128)} fusion(f32[30,16,128]{2,0,1:T(8,128)S(1)} %copy.78, f32[32,30,16,128]{3,1,2,0:T(8,128)} %copy-done.3, f32[32,30,1,128]{3,1,2,0:T(8,128)S(1)} %collective-permute-done.1, f32[32,30,1,128]{3,1,2,0:T(8,128)S(1)} %collective-permute-done, f32[32,30,16,127]{3,1,2,0:T(8,128)} %get-tuple-element.44, ...), kind=kOutput, calls=%fused_computation.4 | convolution fusion | flops 739246080 | bytes 32697872 | tf_op jit(solution)/shard_map/ij,mjac->miac/dot_general | solution.py:33
  66.5 13.0 %fusion.120 = (f32[32,30,16,127]{3,1,2,0:T(8,128)}, f32[32,30,16,127]{3,1,2,0:T(8,128)}) fusion(f32[32,30,16,128]{3,1,2,0:T(8,128)} %fusion), kind=kLoop, calls=%fused_computation.153 | loop fusion | bytes 31211520 | tf_op jit(solution)/shard_map/jit(_roll_static)/slice | solution.py:29
  80.8 5.7 %collective-permute-start.3 = (f32[32,30,1,128]{3,1,2,0:T(8,128)S(1)}, f32[32,30,1,128]{3,1,2,0:T(8,128)S(1)}, u32[]{:S(2)}, u32[]{:S(2)}) collective-permute-start(f32[32,30,1,128]{3,1,2,0:T(8,128)S(1)} %get-tuple-element.42), channel_id=1, source_target_pairs={{0,8},{8,16},{16,24},{1,9},{9,17},{17,25},{2,10},{10,18},{18,26},{... | collective-permute-start | bytes 1474568 | tf_op jit(solution)/shard_map/ppermute | solution.py:17
  86.5 7.3 %fusion.121 = (f32[32,30,16,1]{3,1,2,0:T(8,128)}, f32[32,30,16,1]{3,1,2,0:T(8,128)}) fusion(f32[32,30,16,128]{3,1,2,0:T(8,128)S(1)} %copy-done.1), kind=kLoop, calls=%fused_computation.154 | loop fusion | bytes 245760 | tf_op jit(solution)/shard_map/jit(_roll_static)/slice | solution.py:29
  97.1 26.8 %fusion.1 = f32[32,30,16,128]{3,1,2,0:T(8,128)} fusion(f32[30,16,128]{2,0,1:T(8,128)S(1)} %copy.78, f32[32,30,16,128]{3,1,2,0:T(8,128)} %fusion, f32[32,30,1,128]{3,1,2,0:T(8,128)S(1)} %collective-permute-done.3, f32[32,30,1,128]{3,1,2,0:T(8,128)S(1)} %collective-permute-done.2, f32[32,30,16,127]{3,1,2,0:T(8,128)} %get-tuple-element.38, ...), kind=kOutput, calls=%fused_computation.5 | convolution fusion | flops 739246080 | bytes 32697872 | tf_op jit(solution)/shard_map/ij,mjac->miac/dot_general | solution.py:33
  123.9 12.8 %fusion.117 = (f32[32,30,16,127]{3,1,2,0:T(8,128)}, f32[32,30,16,127]{3,1,2,0:T(8,128)}) fusion(f32[32,30,16,128]{3,1,2,0:T(8,128)} %fusion.1), kind=kLoop, calls=%fused_computation.150 | loop fusion | bytes 31211520 | tf_op jit(solution)/shard_map/jit(_roll_static)/slice | solution.py:29
  138.1 12.1 %collective-permute-start.5 = (f32[32,30,1,128]{3,1,2,0:T(8,128)S(1)}, f32[32,30,1,128]{3,1,2,0:T(8,128)S(1)}, u32[]{:S(2)}, u32[]{:S(2)}) collective-permute-start(f32[32,30,1,128]{3,1,2,0:T(8,128)S(1)} %get-tuple-element.36), channel_id=1, source_target_pairs={{0,8},{8,16},{16,24},{1,9},{9,17},{17,25},{2,10},{10,18},{18,26},{... | collective-permute-start | bytes 1474568 | tf_op jit(solution)/shard_map/ppermute | solution.py:17
  150.2 7.3 %fusion.118 = (f32[32,30,16,1]{3,1,2,0:T(8,128)}, f32[32,30,16,1]{3,1,2,0:T(8,128)}) fusion(f32[32,30,16,128]{3,1,2,0:T(8,128)S(1)} %copy-done.2), kind=kLoop, calls=%fused_computation.151 | loop fusion | bytes 245760 | tf_op jit(solution)/shard_map/jit(_roll_static)/slice | solution.py:29
  160.8 26.9 %fusion.2 = f32[32,30,16,128]{3,1,2,0:T(8,128)} fusion(f32[30,16,128]{2,0,1:T(8,128)S(1)} %copy.78, f32[32,30,16,128]{3,1,2,0:T(8,128)} %fusion.1, f32[32,30,1,128]{3,1,2,0:T(8,128)S(1)} %collective-permute-done.5, f32[32,30,1,128]{3,1,2,0:T(8,128)S(1)} %collective-permute-done.4, f32[32,30,16,127]{3,1,2,0:T(8,128)} %get-tuple-element.32, ...), kind=kOutput, calls=%fused_computation.6 | convolution fusion | flops 739246080 | bytes 32697872 | tf_op jit(solution)/shard_map/ij,mjac->miac/dot_general | solution.py:33
  187.7 13.0 %fusion.114 = (f32[32,30,16,127]{3,1,2,0:T(8,128)}, f32[32,30,16,127]{3,1,2,0:T(8,128)}) fusion(f32[32,30,16,128]{3,1,2,0:T(8,128)} %fusion.2), kind=kLoop, calls=%fused_computation.147 | loop fusion | bytes 31211520 | tf_op jit(solution)/shard_map/jit(_roll_static)/slice | solution.py:29
  202.1 11.7 %collective-permute-start.7 = (f32[32,30,1,128]{3,1,2,0:T(8,128)S(1)}, f32[32,30,1,128]{3,1,2,0:T(8,128)S(1)}, u32[]{:S(2)}, u32[]{:S(2)}) collective-permute-start(f32[32,30,1,128]{3,1,2,0:T(8,128)S(1)} %get-tuple-element.30), channel_id=1, source_target_pairs={{0,8},{8,16},{16,24},{1,9},{9,17},{17,25},{2,10},{10,18},{18,26},{... | collective-permute-start | bytes 1474568 | tf_op jit(solution)/shard_map/ppermute | solution.py:17
  213.8 7.3 %fusion.115 = (f32[32,30,16,1]{3,1,2,0:T(8,128)}, f32[32,30,16,1]{3,1,2,0:T(8,128)}) fusion(f32[32,30,16,128]{3,1,2,0:T(8,128)S(1)} %copy-done.4), kind=kLoop, calls=%fused_computation.148 | loop fusion | bytes 245760 | tf_op jit(solution)/shard_map/jit(_roll_static)/slice | solution.py:29
  224.3 27.2 %multiply_reduce_fusion = (f32[30,16,128]{2,0,1:T(8,128)S(1)}, f32[32,30,16,128]{3,1,2,0:T(8,128)}) fusion(f32[32]{0:T(128)S(1)} %compare_convert_fusion, f32[30,16,128]{2,0,1:T(8,128)S(1)} %copy.78, f32[30,30]{1,0:T(8,128)S(1)} %copy-done.7, f32[32,30,16,128]{3,1,2,0:T(8,128)} %fusion.2, f32[32,30,1,128]{3,1,2,0:T(8,128)S(1)} %collective-permute-done.7, ...), kind=kOutput, calls=%fused_computation.83 | convolution fusion | flops 743116800 | bytes 32943760 | tf_op jit(solution)/shard_map/ij,mjac->miac/dot_general | solution.py:33
  255.7 9.9 %collective-permute-start.8 = (f32[32,3,1,128]{3,1,2,0:T(4,128)S(1)}, f32[32,3,1,128]{3,1,2,0:T(4,128)S(1)}, u32[]{:S(2)}, u32[]{:S(2)}) collective-permute-start(f32[32,3,1,128]{3,1,2,0:T(4,128)S(1)} %get-tuple-element.58), channel_id=1, source_target_pairs={{0,8},{8,16},{16,24},{1,9},{9,17},{17,25},{2,10},{10,18},{18,26},{... | collective-permute-start | bytes 147464 | tf_op jit(solution)/shard_map/ppermute | solution.py:17
  288.1 8.5 %reshape.33 = f32[32,27,2048]{2,1,0:T(8,128)} reshape(f32[32,3,9,16,128]{4,3,2,1,0:T(8,128)} %copy.87) | data formatting | bytes 14155776 | tf_op jit(solution)/shard_map/reshape | solution.py:51
  296.6 13.6 %maximum_bitcast_fusion = f32[32,32,2048]{2,1,0:T(8,128)S(1)} fusion(f32[32,27,2048]{2,1,0:T(8,128)} %reshape.33, f32[32,27]{1,0:T(8,128)S(1)} %copy-done.11), kind=kOutput, calls=%fused_computation.82 | convolution fusion | flops 681574400 | bytes 15469952 | tf_op jit(solution)/shard_map/ck,mkp->mcp/dot_general | solution.py:53
  310.2 10.7 %fusion.90 = f32[32]{0:T(128)S(1)} fusion(f32[32,2048,1]{1,2,0:T(1,128)S(1)} %bitcast.83, f32[32,32,2048]{2,1,0:T(8,128)S(1)} %maximum_bitcast_fusion), kind=kOutput, calls=%fused_computation.99 | convolution fusion | flops 25165824 | bytes 8650880 | tf_op jit(solution)/shard_map/mcp,cp->m/dot_general | solution.py:55
  320.9 10.8 %psum.7 = f32[32]{0:T(128)S(1)} all-reduce(f32[32]{0:T(128)S(1)} %fusion.90), channel_id=1, replica_groups=mesh['lat'=4,'grp'=8] {'lat'}, use_global_device_ids=true, to_apply=%region_2.3 | all-reduce | flops 32 | bytes 256 | tf_op jit(solution)/shard_map/psum | solution.py:83
  332.0 13.8 %all-reduce = f32[256]{0:T(256)S(1)} all-reduce(f32[256]{0:T(256)S(1)} %dynamic-update-slice), channel_id=1, replica_groups=mesh['lat'=4,'grp'=8] {'grp'}, use_global_device_ids=true, to_apply=%add | all-reduce | flops 256 | bytes 2048
  353.5 10.3 %copy.83 = f32[32,30,16,128]{3,2,1,0:T(8,128)} copy(f32[32,30,16,128]{3,1,2,0:T(8,128)S(1)} %broadcast_select_fusion) | data formatting | bytes 15728640
  (90 shorter events, 50.6 us)
Async XLA Ops:
  7.2 303.1 %copy-start = (f32[32,16,128]{2,1,0:T(8,128)S(1)}, f32[32,16,128]{2,1,0:T(8,128)}, u32[]{:S(2)}) copy-start(f32[32,16,128]{2,1,0:T(8,128)} %param.15) | copy-start | bytes 786436
  7.2 340.7 %all-gather.3.cloned.1.call-start = ((), (), s32[]{:S(2)}) async-start(), calls=%async_computation | async-start | bytes 2211840 | tf_op jit(solution)/shard_map/all_gather | solution.py:74
  13.7 14.3 %copy-start.3 = (f32[32,30,16,128]{3,1,2,0:T(8,128)}, f32[32,30,16,128]{3,1,2,0:T(8,128)S(1)}, u32[]{:S(2)}) copy-start(f32[32,30,16,128]{3,1,2,0:T(8,128)S(1)} %copy.77) | copy-start | bytes 23592964
  13.8 25.7 %collective-permute-start = (f32[32,30,1,128]{3,1,2,0:T(8,128)S(1)}, f32[32,30,1,128]{3,1,2,0:T(8,128)S(1)}, u32[]{:S(2)}, u32[]{:S(2)}) collective-permute-start(f32[32,30,1,128]{3,1,2,0:T(8,128)S(1)} %get-tuple-element.47), channel_id=1, source_target_pairs={{8,0},{16,8},{24,16},{9,1},{17,9},{25,17},{10,2},{18,10},{26,18},{... | collective-permute-start | bytes 1474568 | tf_op jit(solution)/shard_map/ppermute | solution.py:18
  15.1 24.4 %collective-permute-start.1 = (f32[32,30,1,128]{3,1,2,0:T(8,128)S(1)}, f32[32,30,1,128]{3,1,2,0:T(8,128)S(1)}, u32[]{:S(2)}, u32[]{:S(2)}) collective-permute-start(f32[32,30,1,128]{3,1,2,0:T(8,128)S(1)} %get-tuple-element.48), channel_id=1, source_target_pairs={{0,8},{8,16},{16,24},{1,9},{9,17},{17,25},{2,10},{10,18},{18,26},{... | collective-permute-start | bytes 1474568 | tf_op jit(solution)/shard_map/ppermute | solution.py:17
  28.0 7.4 %copy-start.8 = (f32[30,16,128]{2,1,0:T(8,128)S(1)}, f32[30,16,128]{2,1,0:T(8,128)}, u32[]{:S(2)}) copy-start(f32[30,16,128]{2,1,0:T(8,128)} %param.12) | copy-start | bytes 737284
  28.0 7.5 %copy-start.10 = (s32[16,128]{1,0:T(8,128)S(1)}, s32[16,128]{1,0:T(8,128)}, u32[]{:S(2)}) copy-start(s32[16,128]{1,0:T(8,128)} %param.13) | copy-start | bytes 24580
  28.0 7.5 %copy-start.12 = (s32[256]{0:T(256)S(1)}, s32[256]{0:T(256)}, u32[]{:S(2)}) copy-start(s32[256]{0:T(256)} %param.16) | copy-start | bytes 3076
  28.1 9.5 %copy-start.14 = (u32[32]{0:T(128)S(1)}, u32[32]{0:T(128)}, u32[]{:S(2)}) copy-start(u32[32]{0:T(128)} %constant.50) | copy-start | bytes 388
  28.1 11.5 %copy-start.7 = (f32[30,30]{1,0:T(8,128)S(1)}, f32[30,30]{1,0:T(8,128)}, u32[]{:S(2)}) copy-start(f32[30,30]{1,0:T(8,128)} %param.11) | copy-start | bytes 10804
  28.1 11.5 %copy-start.9 = (f32[16,128]{1,0:T(8,128)S(1)}, f32[16,128]{1,0:T(8,128)}, u32[]{:S(2)}) copy-start(f32[16,128]{1,0:T(8,128)} %param.10) | copy-start | bytes 24580
  66.5 13.0 %copy-start.1 = (f32[32,30,16,128]{3,1,2,0:T(8,128)S(1)}, f32[32,30,16,128]{3,1,2,0:T(8,128)}, u32[]{:S(2)}) copy-start(f32[32,30,16,128]{3,1,2,0:T(8,128)} %fusion) | copy-start | bytes 23592964
  79.5 17.6 %collective-permute-start.2 = (f32[32,30,1,128]{3,1,2,0:T(8,128)S(1)}, f32[32,30,1,128]{3,1,2,0:T(8,128)S(1)}, u32[]{:S(2)}, u32[]{:S(2)}) collective-permute-start(f32[32,30,1,128]{3,1,2,0:T(8,128)S(1)} %get-tuple-element.41), channel_id=1, source_target_pairs={{8,0},{16,8},{24,16},{9,1},{17,9},{25,17},{10,2},{18,10},{26,18},{... | collective-permute-start | bytes 1474568 | tf_op jit(solution)/shard_map/ppermute | solution.py:18
  80.8 16.3 %collective-permute-start.3 = (f32[32,30,1,128]{3,1,2,0:T(8,128)S(1)}, f32[32,30,1,128]{3,1,2,0:T(8,128)S(1)}, u32[]{:S(2)}, u32[]{:S(2)}) collective-permute-start(f32[32,30,1,128]{3,1,2,0:T(8,128)S(1)} %get-tuple-element.42), channel_id=1, source_target_pairs={{0,8},{8,16},{16,24},{1,9},{9,17},{17,25},{2,10},{10,18},{18,26},{... | collective-permute-start | bytes 1474568 | tf_op jit(solution)/shard_map/ppermute | solution.py:17
  123.9 12.8 %copy-start.2 = (f32[32,30,16,128]{3,1,2,0:T(8,128)S(1)}, f32[32,30,16,128]{3,1,2,0:T(8,128)}, u32[]{:S(2)}) copy-start(f32[32,30,16,128]{3,1,2,0:T(8,128)} %fusion.1) | copy-start | bytes 23592964
  136.8 24.0 %collective-permute-start.4 = (f32[32,30,1,128]{3,1,2,0:T(8,128)S(1)}, f32[32,30,1,128]{3,1,2,0:T(8,128)S(1)}, u32[]{:S(2)}, u32[]{:S(2)}) collective-permute-start(f32[32,30,1,128]{3,1,2,0:T(8,128)S(1)} %get-tuple-element.35), channel_id=1, source_target_pairs={{8,0},{16,8},{24,16},{9,1},{17,9},{25,17},{10,2},{18,10},{26,18},{... | collective-permute-start | bytes 1474568 | tf_op jit(solution)/shard_map/ppermute | solution.py:18
  138.1 22.7 %collective-permute-start.5 = (f32[32,30,1,128]{3,1,2,0:T(8,128)S(1)}, f32[32,30,1,128]{3,1,2,0:T(8,128)S(1)}, u32[]{:S(2)}, u32[]{:S(2)}) collective-permute-start(f32[32,30,1,128]{3,1,2,0:T(8,128)S(1)} %get-tuple-element.36), channel_id=1, source_target_pairs={{0,8},{8,16},{16,24},{1,9},{9,17},{17,25},{2,10},{10,18},{18,26},{... | collective-permute-start | bytes 1474568 | tf_op jit(solution)/shard_map/ppermute | solution.py:17
  187.7 13.0 %copy-start.4 = (f32[32,30,16,128]{3,1,2,0:T(8,128)S(1)}, f32[32,30,16,128]{3,1,2,0:T(8,128)}, u32[]{:S(2)}) copy-start(f32[32,30,16,128]{3,1,2,0:T(8,128)} %fusion.2) | copy-start | bytes 23592964
  200.8 23.4 %collective-permute-start.6 = (f32[32,30,1,128]{3,1,2,0:T(8,128)S(1)}, f32[32,30,1,128]{3,1,2,0:T(8,128)S(1)}, u32[]{:S(2)}, u32[]{:S(2)}) collective-permute-start(f32[32,30,1,128]{3,1,2,0:T(8,128)S(1)} %get-tuple-element.29), channel_id=1, source_target_pairs={{8,0},{16,8},{24,16},{9,1},{17,9},{25,17},{10,2},{18,10},{26,18},{... | collective-permute-start | bytes 1474568 | tf_op jit(solution)/shard_map/ppermute | solution.py:18
  202.1 22.1 %collective-permute-start.7 = (f32[32,30,1,128]{3,1,2,0:T(8,128)S(1)}, f32[32,30,1,128]{3,1,2,0:T(8,128)S(1)}, u32[]{:S(2)}, u32[]{:S(2)}) collective-permute-start(f32[32,30,1,128]{3,1,2,0:T(8,128)S(1)} %get-tuple-element.30), channel_id=1, source_target_pairs={{0,8},{8,16},{16,24},{1,9},{9,17},{17,25},{2,10},{10,18},{18,26},{... | collective-permute-start | bytes 1474568 | tf_op jit(solution)/shard_map/ppermute | solution.py:17
  255.7 14.4 %collective-permute-start.8 = (f32[32,3,1,128]{3,1,2,0:T(4,128)S(1)}, f32[32,3,1,128]{3,1,2,0:T(4,128)S(1)}, u32[]{:S(2)}, u32[]{:S(2)}) collective-permute-start(f32[32,3,1,128]{3,1,2,0:T(4,128)S(1)} %get-tuple-element.58), channel_id=1, source_target_pairs={{0,8},{8,16},{16,24},{1,9},{9,17},{17,25},{2,10},{10,18},{18,26},{... | collective-permute-start | bytes 147464 | tf_op jit(solution)/shard_map/ppermute | solution.py:17
  265.6 7.5 %collective-permute-start.9 = (f32[32,3,1,128]{3,1,2,0:T(4,128)S(1)}, f32[32,3,1,128]{3,1,2,0:T(4,128)S(1)}, u32[]{:S(2)}, u32[]{:S(2)}) collective-permute-start(f32[32,3,1,128]{3,1,2,0:T(4,128)S(1)} %get-tuple-element.57), channel_id=1, source_target_pairs={{8,0},{16,8},{24,16},{9,1},{17,9},{25,17},{10,2},{18,10},{26,18},{... | collective-permute-start | bytes 147464 | tf_op jit(solution)/shard_map/ppermute | solution.py:18
  288.1 8.5 %copy-start.11 = (f32[32,27]{1,0:T(8,128)S(1)}, f32[32,27]{1,0:T(8,128)}, u32[]{:S(2)}) copy-start(f32[32,27]{1,0:T(8,128)} %param.14) | copy-start | bytes 10372
  331.8 21.7 %copy-start.15 = (f32[32]{0:T(128)}, f32[32]{0:T(128)S(1)}, u32[]{:S(2)}) copy-start(f32[32]{0:T(128)S(1)} %psum.7) | copy-start | bytes 388
  (3 other events, 14.4 us)
Sparse Core Ops, SparseCore 0:
  270.2 33.2 all-gather.2
where the time goes:
time: 375 us; the launch traced here: 371 us
  matrix products  132 us (35%)
  local copies, waits for them, and re-layouts  114 us (30%)
  starting transfers between devices  51.8 us (14%)
  blocking collectives  24.7 us (7%)
  between operations  18.2 us (5%)
  other arithmetic  17.4 us (5%)
  waiting for transfers between devices  12.9 us (3%)
    dot_general x4, matrix products, advance(): jnp.einsum('ij,mjac->miac', mixing, smooth, precision=lax.Precision.HIGHEST)  108 us
    slice x8, local copies, waits for them, and re-layouts, advance(): jnp.roll(values, -1, 3)  75.2 us
    ppermute x5, starting transfers between devices, with_halo(): before = lax.ppermute(last, axis, up)  45.1 us
    unnamed x40, local copies, waits for them, and re-layouts  18.5 us
    unnamed x1, blocking collectives  13.8 us
    dot_general x1, matrix products, score_terms(): jnp.einsum('ck,mkp->mcp', conv_weight, patches, precision=lax.Precision.H...  13.6 us
    ppermute x5, waiting for transfers between devices, with_halo(): after = lax.ppermute(initial, axis, down)  12.9 us
    reshape x2, local copies, waits for them, and re-layouts, score_terms(): jnp.stack(taps, 2).reshape(members_here, 27, height * padded.shape[3])  12.2 us
  transfers between devices with their start and end apart: 11, of which 4 were waited for; matrix products, arithmetic and copies ran while one was open for 24% of the time, Pallas kernels for 0%

commit v1 on v0

v1 whole, which is shorter than its diff:
```python
import functools
import jax
import jax.numpy as jnp
from jax import lax
from jax.experimental import pallas as pl
from jax.experimental.pallas import tpu as pltpu
from jax.sharding import PartitionSpec as P

LEV = 10
STEPS = 4
SUB = 8
CHUNKS = 4
EXT = 2 * STEPS
F32 = jnp.float32
BF16 = jnp.bfloat16


def split_hi_lo(value):
    hi = value.astype(BF16)
    lo = (value - hi.astype(F32)).astype(BF16)
    return hi, lo


def split_constant(value):
    hi = lax.reduce_precision(value, 8, 7)
    return hi.astype(BF16), (value - hi).astype(BF16)


def dot3(a_hi, a_lo, b_hi, b_lo):
    dot = functools.partial(jnp.dot, preferred_element_type=F32)
    return dot(a_hi, b_hi) + (dot(a_hi, b_lo) + dot(a_lo, b_hi))


def steps_body(fields_ref, below_ref, above_ref, diff_ref, heat_ref, w_hi_ref, w_lo_ref, x_ref, y_hi_ref, y_lo_ref):
    members, levels, rows, lon = x_ref.shape
    own = rows - EXT
    tiles = rows // SUB
    width = members * tiles * lon
    cols = min(2 * lon, width)
    x_ref[:, :, :own, :] = fields_ref[...]
    x_ref[:, :, own : own + STEPS, :] = below_ref[...]
    x_ref[:, :, own + STEPS :, :] = above_ref[...]
    place = lax.broadcasted_iota(jnp.int32, (1, SUB, lon), 1)
    depth = jnp.where(place < STEPS, place, SUB - 1 - place)

    def one_step(step, carry):
        for g in range(members):
            for f in range(0, levels, 2):
                x = x_ref[g, f : f + 2]
                near = (
                    pltpu.roll(x, 1, 1)
                    + pltpu.roll(x, rows - 1, 1)
                    + pltpu.roll(x, 1, 2)
                    + pltpu.roll(x, lon - 1, 2)
                    - 4.0 * x
                )
                y = x + diff_ref[...][None] * near
                for t in range(tiles):
                    part = y[:, SUB * t : SUB * (t + 1), :].reshape(2 * SUB, lon)
                    hi, lo = split_hi_lo(part)
                    at = (g * tiles + t) * lon
                    y_hi_ref[SUB * f : SUB * (f + 2), at : at + lon] = hi
                    y_lo_ref[SUB * f : SUB * (f + 2), at : at + lon] = lo
        for start in range(0, width, cols):
            end = min(start + cols, width)
            z = dot3(w_hi_ref[...], w_lo_ref[...], y_hi_ref[:, start:end], y_lo_ref[:, start:end])
            for at in range(start, end, lon):
                g, t = divmod(at // lon, tiles)
                mixed = z[:, at - start : at - start + lon].reshape(levels, SUB, lon)
                new = mixed + heat_ref[:, SUB * t : SUB * (t + 1), :] - 0.05 * mixed * mixed * mixed
                if t == tiles - 1:
                    new = jnp.where(depth < STEPS - 1 - step, new, 0.0)
                x_ref[g, :, SUB * t : SUB * (t + 1), :] = new
        return carry

    lax.fori_loop(0, STEPS, one_step, 0)


def donor_kernel(fields_ref, below_ref, above_ref, diff_ref, heat_ref, w_hi_ref, w_lo_ref, out_ref, x_ref, y_hi_ref, y_lo_ref):
    steps_body(fields_ref, below_ref, above_ref, diff_ref, heat_ref, w_hi_ref, w_lo_ref, x_ref, y_hi_ref, y_lo_ref)
    out_ref[...] = x_ref[:, :, : out_ref.shape[2], :]


def chunk_kernel(first, killed_ref, fields_ref, below_ref, above_ref, donor_ref, diff_ref, heat_ref, w_hi_ref, w_lo_ref, *rest):
    out_ref, tq_ref, x_ref, y_hi_ref, y_lo_ref = rest[-5:]
    steps_body(fields_ref, below_ref, above_ref, diff_ref, heat_ref, w_hi_ref, w_lo_ref, x_ref, y_hi_ref, y_lo_ref)
    members, levels, own, lon = out_ref.shape
    for g in range(members):
        tq_ref[g, 0] = x_ref[g, 0, :own, :]
        tq_ref[g, 1] = x_ref[g, LEV, :own, :]
        killed = killed_ref[first + pl.program_id(0) * members + g] != 0

        @pl.when(killed)
        def _():
            out_ref[g] = donor_ref[0]

        @pl.when(jnp.logical_not(killed))
        def _():
            out_ref[g] = x_ref[g, :, :own, :]


def score_kernel(tq_ref, ext_ref, land_ref, b_hi_ref, b_lo_ref, head_ref, out_ref):
    members, _, own, lon = tq_ref.shape
    land = land_ref[...]
    depth = b_hi_ref.shape[1]
    pad = depth - 9 * (own + SUB)
    highs, lows = [], []
    for g in range(members):
        t = jnp.concatenate([tq_ref[g, 0], ext_ref[g, 0]], axis=0)
        q = jnp.concatenate([tq_ref[g, 1], ext_ref[g, 1]], axis=0)
        rows = []
        for value in (t * land, q, t * (1.0 - land)):
            rows += [pltpu.roll(value, 1, 1), value, pltpu.roll(value, lon - 1, 1)]
        if pad:
            rows.append(jnp.zeros((pad, lon), F32))
        hi, lo = split_hi_lo(jnp.concatenate(rows, axis=0))
        highs.append(hi)
        lows.append(lo)
    for g in range(0, members, 2):
        hidden = dot3(
            b_hi_ref[...],
            b_lo_ref[...],
            jnp.concatenate(highs[g : g + 2], axis=1),
            jnp.concatenate(lows[g : g + 2], axis=1),
        )
        hidden = jnp.maximum(hidden, 0.0)
        for k in range(2):
            terms = hidden[:, k * lon : (k + 1) * lon] * head_ref[...]
            out_ref[g + k : g + k + 1, :] = jnp.sum(terms, axis=0, keepdims=True)


def params():
    return pltpu.CompilerParams(vmem_limit_bytes=40 * 2**20)


def full_spec(array):
    zeros = (0,) * array.ndim
    return pl.BlockSpec(array.shape, lambda *_: zeros)


def steps_scratch(members, levels, rows, lon):
    width = members * (rows // SUB) * lon
    return [
        pltpu.VMEM((members, levels, rows, lon), F32),
        pltpu.VMEM((levels * SUB, width), BF16),
        pltpu.VMEM((levels * SUB, width), BF16),
    ]


def run_donor(donor, below, above, consts):
    _, levels, own, lon = donor.shape
    ins = (donor, below, above) + consts
    return pl.pallas_call(
        donor_kernel,
        out_shape=jax.ShapeDtypeStruct(donor.shape, F32),
        in_specs=[full_spec(a) for a in ins],
        out_specs=full_spec(donor),
        grid=(1,),
        scratch_shapes=steps_scratch(1, levels, own + EXT, lon),
        compiler_params=params(),
        name="donor_steps",
    )(*ins)


def run_chunk(index, size, killed, fields, below, above, donor, consts, held):
    members, levels, own, lon = fields.shape
    group = 2
    blocks = size // group
    first = index * size
    block = pl.BlockSpec((group, levels, own, lon), lambda i: (i + index * blocks, 0, 0, 0))
    halo = pl.BlockSpec((group, levels, STEPS, lon), lambda i: (i, 0, 0, 0))
    ins = [killed, fields, below, above, donor, *consts]
    in_specs = [pl.BlockSpec(memory_space=pltpu.SMEM), block, halo, halo, full_spec(donor)]
    in_specs += [full_spec(a) for a in consts]
    alias = {}
    if held is not None:
        alias = {len(ins): 0}
        ins.append(held)
        in_specs.append(pl.BlockSpec(memory_space=pl.ANY))
    flops = 6 * size * levels * levels * SUB * (own + EXT) * lon * STEPS
    return pl.pallas_call(
        functools.partial(chunk_kernel, first),
        out_shape=(
            jax.ShapeDtypeStruct(fields.shape, F32),
            jax.ShapeDtypeStruct((size, 2, own, lon), F32),
        ),
        in_specs=in_specs,
        out_specs=(block, pl.BlockSpec((group, 2, own, lon), lambda i: (i, 0, 0, 0))),
        grid=(blocks,),
        scratch_shapes=steps_scratch(group, levels, own + EXT, lon),
        input_output_aliases=alias,
        compiler_params=params(),
        cost_estimate=pl.CostEstimate(flops=flops, bytes_accessed=2 * size * levels * own * lon * 4, transcendentals=0),
        name="chunk_steps",
    )(*ins)


def run_scores(tq, ext, land, b_hi, b_lo, head):
    members, _, own, lon = tq.shape
    group = 8
    return pl.pallas_call(
        score_kernel,
        out_shape=jax.ShapeDtypeStruct((members, lon), F32),
        in_specs=[
            pl.BlockSpec((group, 2, own, lon), lambda i: (i, 0, 0, 0)),
            pl.BlockSpec((group, 2, SUB, lon), lambda i: (i, 0, 0, 0)),
            full_spec(land),
            full_spec(b_hi),
            full_spec(b_lo),
            full_spec(head),
        ],
        out_specs=pl.BlockSpec((group, lon), lambda i: (i, 0)),
        grid=(members // group,),
        compiler_params=params(),
        name="score_terms",
    )(tq, ext, land, b_hi, b_lo, head)


def halos(value, dim, width, axis="lat"):
    size, length = lax.axis_size(axis), value.shape[dim]
    up = [(i, i + 1) for i in range(size - 1)]
    down = [(j, i) for i, j in up]
    above = lax.ppermute(lax.slice_in_dim(value, length - width, length, axis=dim), axis, up)
    below = lax.ppermute(lax.slice_in_dim(value, 0, width, axis=dim), axis, down)
    return below, above


def conv_matrix(conv_weight, own):
    rows = own + SUB
    channels = conv_weight.shape[0]
    taps = conv_weight.reshape(channels, 1, 3, 3, 3, 1)
    i = jnp.arange(own)[:, None, None]
    a = jnp.arange(3)[None, :, None]
    r = jnp.arange(rows)[None, None, :]
    hit = ((i + a - 1) % rows == r).astype(F32)
    parts = [taps[:, :, :, k] * hit[None, :, None, None, k, :] for k in range(3)]
    matrix = (parts[0] + parts[1] + parts[2]).reshape(channels * own, 9 * rows)
    pad = -matrix.shape[1] % 16
    return jnp.pad(matrix, ((0, 0), (0, pad)))


def local(fields, diffusion, mixing, heating, land_mask, conv_weight, head_weight, counts, source):
    members, levels, own, lon = fields.shape
    total_members = counts.shape[0]
    me = lax.axis_index("grp")
    offset = me * members
    local_counts = lax.dynamic_slice_in_dim(counts, offset, members)
    local_source = lax.dynamic_slice_in_dim(source, offset, members)
    killed = (local_source != offset + jnp.arange(members, dtype=jnp.int32)).astype(jnp.int32)
    donor_group = jnp.max(jnp.where(killed > 0, local_source // members, 0))

    hot = lax.dynamic_index_in_dim(fields, jnp.argmax(local_counts), 0, keepdims=False)
    hot_all = jnp.concatenate([hot, *halos(hot, 1, STEPS)], axis=1)
    gathered = lax.all_gather(hot_all, "grp", axis=0)
    donor_all = lax.dynamic_index_in_dim(gathered, donor_group, 0, keepdims=True)

    diff_all = jnp.concatenate([diffusion, *halos(diffusion, 0, STEPS)], axis=0)
    heat_all = jnp.concatenate([heating, *halos(heating, 1, STEPS)], axis=1)
    eye = jnp.eye(SUB, dtype=F32)
    wide = (mixing[:, None, :, None] * eye[None, :, None, :]).reshape(levels * SUB, levels * SUB)
    consts = (diff_all, heat_all, *split_constant(wide))

    donor = run_donor(
        donor_all[:, :, :own],
        donor_all[:, :, own : own + STEPS],
        donor_all[:, :, own + STEPS :],
        consts,
    )
    size = members // CHUNKS
    held, parts = None, []
    for c in range(CHUNKS):
        piece = lax.slice_in_dim(fields, c * size, (c + 1) * size, axis=0)
        below, above = halos(piece, 2, STEPS)
        held, tq = run_chunk(c, size, killed, fields, below, above, donor, consts, held)
        parts.append(tq)
    tq = jnp.concatenate(parts, axis=0)

    land = land_mask.astype(F32)
    land_below, land_above = halos(land, 0, 1)
    land_all = jnp.concatenate([land, land_below, jnp.zeros((SUB - 2, lon), F32), land_above], axis=0)
    tq_below, tq_above = halos(tq, 2, 1)
    ext = jnp.concatenate([tq_below, jnp.zeros((members, 2, SUB - 2, lon), F32), tq_above], axis=2)
    b_hi, b_lo = split_constant(conv_matrix(conv_weight, own))
    partial = run_scores(tq, ext, land_all, b_hi, b_lo, head_weight.reshape(-1, lon))
    partial = jnp.sum(partial, axis=1)
    everything = lax.all_gather(partial, ("lat", "grp"), axis=0)
    all_scores = everything.reshape(lax.axis_size("lat"), total_members).sum(0)
    scores = lax.dynamic_slice_in_dim(all_scores, offset, members)
    weights = jnp.exp(all_scores)
    weights = weights / jnp.mean(weights)
    selector = (local_source[:, None] == jnp.arange(total_members, dtype=jnp.int32)[None, :]).astype(F32)
    chosen_weight = jnp.sum(selector * weights[None, :], 1)
    chosen_count = jnp.sum(selector * counts.astype(F32)[None, :], 1)
    return held, scores, chosen_weight / chosen_count


def solution(mesh):
    return jax.shard_map(
        local,
        mesh=mesh,
        in_specs=(
            P("grp", None, "lat", None),
            P("lat", None),
            P(),
            P(None, "lat", None),
            P("lat", None),
            P(),
            P(None, "lat", None),
            P(),
            P(),
        ),
        out_specs=(P("grp", None, "lat", None), P("grp"), P("grp")),
        check_vma=False,
    )
```

time: 375 us -> 240 us (0.64)
  matrix products: 132 us -> 0 us
  local copies, waits for them, and re-layouts: 114 us -> 20.3 us
  Pallas kernels: 0 us -> 75.7 us
  blocking collectives: 24.7 us -> 40.5 us
  starting transfers between devices: 51.8 us -> 61.2 us
  other arithmetic: 17.4 us -> 9.79 us
    dot_general x6 -> x0, matrix products: 132 us -> none  [the longest x4 108 us: advance(): jnp.einsum('ij,mjac->miac', mixing, smooth, precision=lax.Precision.HIGHEST)]
    pallas_call x0 -> x6, Pallas kernels: none -> 75.7 us  [the longest x4 68.7 us: run_chunk(): pl.pallas_call(functools.partial(chunk_kernel, first), out_shape=(jax.Sha...]
    slice x17 -> x8, local copies, waits for them, and re-layouts: 81.6 us -> 7.45 us  [the longest x1 5.36 us: halos(): lax.slice_in_dim(value, length - width, length, axis=dim)]
    unnamed x1, blocking collectives: 13.8 us -> 40.5 us
    unnamed x40 -> x26, local copies, waits for them, and re-layouts: 18.5 us -> 3.64 us
    reshape x2, local copies, waits for them, and re-layouts: 12.2 us -> 0.02 us  [the longest x1 0.01 us: conv_matrix(): taps = conv_weight.reshape(channels, 1, 3, 3, 3, 1)]
    psum x1 -> x0, blocking collectives: 10.8 us -> none  [local(): scores = lax.psum(partial_terms, 'lat')]
    ppermute x10 -> x18, starting transfers between devices: 51.7 us -> 61.1 us  [the longest x9 49.5 us: halos(): lax.ppermute(lax.slice_in_dim(value, length - width, length, axis=dim), a...]
  transfers between devices with their start and end apart: 11 -> 19, of which waited for: 4 -> 7; matrix products, arithmetic and copies ran while one was open for 24% -> 9% of each run, Pallas kernels for 0% -> 30%
where the time goes in v1:
time: 240 us; the launch traced here: 239 us
  Pallas kernels  75.7 us (32%)
  starting transfers between devices  61.2 us (26%)
  blocking collectives  40.5 us (17%)
  local copies, waits for them, and re-layouts  20.3 us (8%)
  between operations  19.1 us (8%)
  waiting for transfers between devices  12.4 us (5%)
  other arithmetic  9.79 us (4%)
    pallas_call x4, Pallas kernels, run_chunk(): pl.pallas_call(functools.partial(chunk_kernel, first), out_shape=(jax.Sha...  68.7 us
    ppermute x9, starting transfers between devices, halos(): lax.ppermute(lax.slice_in_dim(value, length - width, length, axis=dim), a...  49.5 us
    unnamed x1, blocking collectives  40.5 us
    ppermute x9, starting transfers between devices, halos(): lax.ppermute(lax.slice_in_dim(value, 0, width, axis=dim), axis, down)  11.6 us
    ppermute x9, waiting for transfers between devices, halos(): lax.ppermute(lax.slice_in_dim(value, 0, width, axis=dim), axis, down)  11.1 us
    slice x1, local copies, waits for them, and re-layouts, halos(): lax.slice_in_dim(value, length - width, length, axis=dim)  5.36 us
  transfers between devices with their start and end apart: 19, of which 7 were waited for; matrix products, arithmetic and copies ran while one was open for 9% of the time, Pallas kernels for 30%

profile of v1, /device:TPU:0, one launch (start us, length us, event | category | flops | bytes accessed | tf_op | source)
XLA Modules:
  0.0 239.0 jit_solution(17355157108005486932)
XLA Ops:
  11.6 4.8 %collective-permute-start.3 = (f32[30,4,128]{2,1,0:T(4,128)S(1)}, f32[30,4,128]{2,1,0:T(4,128)S(1)}, u32[]{:S(2)}, u32[]{:S(2)}) collective-permute-start(f32[30,4,128]{2,1,0:T(4,128)S(1)} %get-tuple-element.44), channel_id=1, source_target_pairs={{0,8},{8,16},{16,24},{1,9},{9,17},{17,25},{2,10},{10,18},{18,26},{... | collective-permute-start | bytes 184328 | tf_op jit(solution)/shard_map/ppermute | solution.py:223
  18.3 4.3 %collective-permute-done.2 = f32[30,4,128]{2,1,0:T(4,128)S(1)} collective-permute-done((f32[30,4,128]{2,1,0:T(4,128)S(1)}, f32[30,4,128]{2,1,0:T(4,128)S(1)}, u32[]{:S(2)}, u32[]{:S(2)}) %collective-permute-start.2) | collective-permute-done | bytes 61472 | tf_op jit(solution)/shard_map/ppermute | solution.py:224
  23.4 5.4 %fusion.8 = (f32[8,30,4,128]{3,2,1,0:T(4,128)}, f32[8,30,4,128]{3,2,1,0:T(4,128)}, f32[8,30,4,128]{3,2,1,0:T(4,128)}, f32[8,30,4,128]{3,2,1,0:T(4,128)}, f32[8,3...) fusion(f32[32,30,16,128]{3,2,1,0:T(8,128)} %fields_ref.7), kind=kLoop, calls=%fused_computation.49 | loop fusion | bytes 7864320 | tf_op jit(solution)/shard_map/slice | solution.py:223
  30.0 4.9 %collective-permute-start.5 = (f32[4,128]{1,0:T(4,128)S(1)}, f32[4,128]{1,0:T(4,128)S(1)}, u32[]{:S(2)}, u32[]{:S(2)}) collective-permute-start(f32[4,128]{1,0:T(4,128)S(1)} %get-tuple-element.54), channel_id=1, source_target_pairs={{0,8},{8,16},{16,24},{1,9},{9,17},{17,25},{2,10},{10,18},{18,26},{... | collective-permute-start | bytes 6152 | tf_op jit(solution)/shard_map/ppermute | solution.py:223
  37.6 6.9 %collective-permute-start.13 = (f32[8,30,4,128]{3,2,1,0:T(4,128)}, f32[8,30,4,128]{3,2,1,0:T(4,128)}, u32[]{:S(2)}, u32[]{:S(2)}) collective-permute-start(f32[8,30,4,128]{3,2,1,0:T(4,128)} %get-tuple-element.25), channel_id=1, source_target_pairs={{0,8},{8,16},{16,24},{1,9},{9,17},{17,25},{2,10},{10,18},{18,26},{... | collective-permute-start | bytes 1474568 | tf_op jit(solution)/shard_map/ppermute | solution.py:223
  44.4 2.5 %broadcast_multiply_fusion = f32[30,8,30,8]{3,2,1,0:T(8,128)} fusion(f32[8,8]{1,0:T(8,128)S(1)} %fusion.3, f32[30,30]{1,0:T(8,128)S(1)} %copy-done.5), kind=kLoop, calls=%fused_computation.1 | loop fusion | flops 57600 | bytes 234256 | tf_op jit(solution)/shard_map/mul | solution.py:260
  46.9 3.7 %mul.97 = f32[240,240]{1,0:T(8,128)S(1)} reshape(f32[30,8,30,8]{3,2,1,0:T(8,128)} %broadcast_multiply_fusion) | data formatting | bytes 460800 | tf_op jit(solution)/shard_map/mul | solution.py:260
  51.2 2.5 %multiply_add_fusion = f32[32,16,3,3,24]{4,3,2,1,0:T(4,128)} fusion(f32[16,24]{1,0:T(8,128)S(1)} %get-tuple-element.46, f32[32,3,3]{2,1,0:T(4,128)S(1)} %copy.26, f32[16,24]{1,0:T(8,128)S(1)} %get-tuple-element.47, f32[32,3,3]{2,1,0:T(4,128)S(1)} %copy.25, f32[16,24]{1,0:T(8,128)S(1)} %get-tuple-element.45, f32[32,3,3]{2,1,0:T(4,128)S(1)} %copy.24), kind=kLoop, calls=%fused_computation | loop fusion | flops 552960 | bytes 450432 | tf_op jit(solution)/shard_map/add | solution.py:237
  53.8 3.4 %add.96 = f32[512,216]{1,0:T(8,128)S(1)} reshape(f32[32,16,3,3,24]{4,3,2,1,0:T(4,128)} %multiply_add_fusion) | data formatting | bytes 884736 | tf_op jit(solution)/shard_map/add | solution.py:237
  60.2 4.1 %collective-permute-start.7 = (f32[30,4,128]{2,1,0:T(4,128)S(1)}, f32[30,4,128]{2,1,0:T(4,128)S(1)}, u32[]{:S(2)}, u32[]{:S(2)}) collective-permute-start(f32[30,4,128]{2,1,0:T(4,128)S(1)} %get-tuple-element.42), channel_id=1, source_target_pairs={{0,8},{8,16},{16,24},{1,9},{9,17},{17,25},{2,10},{10,18},{18,26},{... | collective-permute-start | bytes 184328 | tf_op jit(solution)/shard_map/ppermute | solution.py:223
  66.2 4.3 %collective-permute-start.1 = (f32[8,30,4,128]{3,2,1,0:T(4,128)}, f32[8,30,4,128]{3,2,1,0:T(4,128)S(1)}, u32[]{:S(2)}, u32[]{:S(2)}) collective-permute-start(f32[8,30,4,128]{3,2,1,0:T(4,128)} %get-tuple-element.31), channel_id=1, source_target_pairs={{0,8},{8,16},{16,24},{1,9},{9,17},{17,25},{2,10},{10,18},{18,26},{... | collective-permute-start | bytes 1474568 | tf_op jit(solution)/shard_map/ppermute | solution.py:223
  74.0 2.5 %donor_steps.1.donor_ref = f32[1,30,16,128]{3,2,1,0:T(8,128)S(1)} custom-call(f32[1,30,16,128]{3,2,1,0:T(8,128)S(1)} %constant_dynamic-slice_fusion.1.fields_ref, f32[1,30,4,128]{3,2,1,0:T(4,128)S(1)} %get-tuple-element.34.below_ref, f32[1,30,4,128]{3,2,1,0:T(4,128)S(1)} %get-tuple-element.33.above_ref, f32[24,128]{1,0:T(8,128)S(1)} %pad_maximum_fusion.3.diff_ref, ...), custom_call_target="tpu_custom_call" | custom-call | tf_op jit(solution)/shard_map/donor_steps/pallas_call | solution.py:153
  77.9 6.7 %collective-permute-start.11 = (f32[8,30,4,128]{3,2,1,0:T(4,128)}, f32[8,30,4,128]{3,2,1,0:T(4,128)S(1)}, u32[]{:S(2)}, u32[]{:S(2)}) collective-permute-start(f32[8,30,4,128]{3,2,1,0:T(4,128)} %get-tuple-element.27), channel_id=1, source_target_pairs={{0,8},{8,16},{16,24},{1,9},{9,17},{17,25},{2,10},{10,18},{18,26},{... | collective-permute-start | bytes 1474568 | tf_op jit(solution)/shard_map/ppermute | solution.py:223
  84.5 3.2 %copy-done = f32[32,30,16,128]{3,2,1,0:T(8,128)S(1)} copy-done((f32[32,30,16,128]{3,2,1,0:T(8,128)S(1)}, f32[32,30,16,128]{3,2,1,0:T(8,128)}, u32[]{:S(2)}) %copy-start) | copy-done | bytes 7864344
  87.8 17.5 %chunk_steps.4 = (f32[32,30,16,128]{3,2,1,0:T(8,128)}, f32[8,2,16,128]{3,2,1,0:T(8,128)S(1)}) custom-call(s32[32]{0:T(128)S(1)} %compare_convert_fusion.killed_ref, f32[32,30,16,128]{3,2,1,0:T(8,128)S(1)} %copy-done, f32[8,30,4,128]{3,2,1,0:T(4,128)S(1)} %collective-permute-done.12.below_ref, f32[8,30,4,128]{3,2,1,0:T(4,128)} %collective-permute-done.13.above_ref, ...), custom_call_target="tpu_custom_call" | custom-call | flops 4246732800 | bytes 3932160 | tf_op jit(solution)/shard_map/chunk_steps/pallas_call | solution.py:181
  106.8 3.3 %collective-permute-start.9 = (f32[8,30,4,128]{3,2,1,0:T(4,128)S(1)}, f32[8,30,4,128]{3,2,1,0:T(4,128)S(1)}, u32[]{:S(2)}, u32[]{:S(2)}) collective-permute-start(f32[8,30,4,128]{3,2,1,0:T(4,128)S(1)} %copy-done.3), channel_id=1, source_target_pairs={{0,8},{8,16},{16,24},{1,9},{9,17},{17,25},{2,10},{10,18},{18,26},{... | collective-permute-start | bytes 1474568 | tf_op jit(solution)/shard_map/ppermute | solution.py:223
  110.1 8.7 %collective-permute-start.17 = (f32[1,128]{1,0:T(1,128)S(1)}, f32[1,128]{1,0:T(1,128)S(1)}, u32[]{:S(2)}, u32[]{:S(2)}) collective-permute-start(f32[1,128]{1,0:T(1,128)S(1)} %get-tuple-element.52), channel_id=1, source_target_pairs={{0,8},{8,16},{16,24},{1,9},{9,17},{17,25},{2,10},{10,18},{18,26},{... | collective-permute-start | bytes 1544 | tf_op jit(solution)/shard_map/ppermute | solution.py:223
  118.8 17.1 %chunk_steps.5 = (f32[32,30,16,128]{3,2,1,0:T(8,128)}, f32[8,2,16,128]{3,2,1,0:T(8,128)S(1)}) custom-call(s32[32]{0:T(128)S(1)} %compare_convert_fusion.killed_ref, f32[32,30,16,128]{3,2,1,0:T(8,128)S(1)} %copy-done, f32[8,30,4,128]{3,2,1,0:T(4,128)S(1)} %collective-permute-done.10.below_ref, ...), custom_call_target="tpu_custom_call", output_to_operand_aliasing={{0}: (9, {})} | custom-call | flops 4246732800 | bytes 3932160 | tf_op jit(solution)/shard_map/chunk_steps/pallas_call | solution.py:181
  137.2 17.1 %chunk_steps.6 = (f32[32,30,16,128]{3,2,1,0:T(8,128)}, f32[8,2,16,128]{3,2,1,0:T(8,128)S(1)}) custom-call(s32[32]{0:T(128)S(1)} %compare_convert_fusion.killed_ref, f32[32,30,16,128]{3,2,1,0:T(8,128)S(1)} %copy-done, f32[8,30,4,128]{3,2,1,0:T(4,128)S(1)} %collective-permute-done.8.below_ref, ...), custom_call_target="tpu_custom_call", output_to_operand_aliasing={{0}: (9, {})} | custom-call | flops 4246732800 | bytes 3932160 | tf_op jit(solution)/shard_map/chunk_steps/pallas_call | solution.py:181
  154.4 17.1 %chunk_steps.7 = (f32[32,30,16,128]{3,2,1,0:T(8,128)}, f32[8,2,16,128]{3,2,1,0:T(8,128)S(1)}) custom-call(s32[32]{0:T(128)S(1)} %compare_convert_fusion.killed_ref, f32[32,30,16,128]{3,2,1,0:T(8,128)S(1)} %copy-done, f32[8,30,4,128]{3,2,1,0:T(4,128)S(1)} %collective-permute-done.below_ref, ...), custom_call_target="tpu_custom_call", output_to_operand_aliasing={{0}: (9, {})} | custom-call | flops 4246732800 | bytes 3932160 | tf_op jit(solution)/shard_map/chunk_steps/pallas_call | solution.py:181
  171.5 5.8 %collective-permute-start.15 = (f32[32,2,1,128]{3,2,1,0:T(1,128)S(1)}, f32[32,2,1,128]{3,2,1,0:T(1,128)S(1)}, u32[]{:S(2)}, u32[]{:S(2)}) collective-permute-start(f32[32,2,1,128]{3,2,1,0:T(1,128)S(1)} %get-tuple-element.38), channel_id=1, source_target_pairs={{0,8},{8,16},{16,24},{1,9},{9,17},{17,25},{2,10},{10,18},{18,26},{... | collective-permute-start | bytes 98312 | tf_op jit(solution)/shard_map/ppermute | solution.py:223
  178.9 5.1 %collective-permute-done.14 = f32[32,2,1,128]{3,2,1,0:T(1,128)S(1)} collective-permute-done((f32[32,2,1,128]{3,2,1,0:T(1,128)S(1)}, f32[32,2,1,128]{3,2,1,0:T(1,128)S(1)}, u32[]{:S(2)}, u32[]{:S(2)}) %collective-permute-start.14) | collective-permute-done | bytes 32800 | tf_op jit(solution)/shard_map/ppermute | solution.py:224
  184.1 4.5 %score_terms.1 = f32[32,128]{1,0:T(8,128)S(1)} custom-call(f32[32,2,16,128]{3,2,1,0:T(8,128)S(1)} %constant_dynamic-update-slice_fusion.tq_ref, f32[32,2,8,128]{3,2,1,0:T(8,128)S(1)} %pad_maximum_fusion.2.ext_ref, f32[24,128]{1,0:T(8,128)S(1)} %pad_maximum_fusion.4.land_ref, bf16[512,224]{1,0:T(8,128)(2,1)S(1)} %get-tuple-element.36.b_hi_ref, ...), custom_call_target="tpu_custom_call" | custom-call | tf_op jit(solution)/shard_map/score_terms/pallas_call | solution.py:201
  189.0 40.5 %all-reduce.1 = f32[1024]{0:T(1024)S(1)} all-reduce(f32[1024]{0:T(1024)S(1)} %dynamic-update-slice), channel_id=3, replica_groups=mesh['lat'=4,'grp'=8] {'lat','grp'}, use_global_device_ids=true, to_apply=%add.1 | all-reduce | flops 1024 | bytes 8192
  (94 shorter events, 24.0 us)
Async XLA Ops:
  7.2 64.8 %all-gather.4.cloned.1.call-start = ((), (), s32[]{:S(2)}) async-start(), calls=%async_computation | async-start | bytes 3317760 | tf_op jit(solution)/shard_map/all_gather | solution.py:254
  11.6 6.7 %collective-permute-start.3 = (f32[30,4,128]{2,1,0:T(4,128)S(1)}, f32[30,4,128]{2,1,0:T(4,128)S(1)}, u32[]{:S(2)}, u32[]{:S(2)}) collective-permute-start(f32[30,4,128]{2,1,0:T(4,128)S(1)} %get-tuple-element.44), channel_id=1, source_target_pairs={{0,8},{8,16},{16,24},{1,9},{9,17},{17,25},{2,10},{10,18},{18,26},{... | collective-permute-start | bytes 184328 | tf_op jit(solution)/shard_map/ppermute | solution.py:223
  16.4 6.1 %collective-permute-start.2 = (f32[30,4,128]{2,1,0:T(4,128)S(1)}, f32[30,4,128]{2,1,0:T(4,128)S(1)}, u32[]{:S(2)}, u32[]{:S(2)}) collective-permute-start(f32[30,4,128]{2,1,0:T(4,128)S(1)} %get-tuple-element.43), channel_id=1, source_target_pairs={{8,0},{16,8},{24,16},{9,1},{17,9},{25,17},{10,2},{18,10},{26,18},{... | collective-permute-start | bytes 184328 | tf_op jit(solution)/shard_map/ppermute | solution.py:224
  23.3 6.7 %copy-start.4 = (f32[16,128]{1,0:T(8,128)S(1)}, f32[16,128]{1,0:T(8,128)}, u32[]{:S(2)}) copy-start(f32[16,128]{1,0:T(8,128)} %param.10) | copy-start | bytes 24580
  23.3 21.1 %copy-start.5 = (f32[30,30]{1,0:T(8,128)S(1)}, f32[30,30]{1,0:T(8,128)}, u32[]{:S(2)}) copy-start(f32[30,30]{1,0:T(8,128)} %param.11) | copy-start | bytes 10804
  28.7 125.6 %collective-permute-start = (f32[8,30,4,128]{3,2,1,0:T(4,128)}, f32[8,30,4,128]{3,2,1,0:T(4,128)S(1)}, u32[]{:S(2)}, u32[]{:S(2)}) collective-permute-start(f32[8,30,4,128]{3,2,1,0:T(4,128)} %get-tuple-element.32), channel_id=1, source_target_pairs={{8,0},{16,8},{24,16},{9,1},{17,9},{25,17},{10,2},{18,10},{26,18},{... | collective-permute-start | bytes 1474568 | tf_op jit(solution)/shard_map/ppermute | solution.py:224
  30.0 30.2 %collective-permute-start.5 = (f32[4,128]{1,0:T(4,128)S(1)}, f32[4,128]{1,0:T(4,128)S(1)}, u32[]{:S(2)}, u32[]{:S(2)}) collective-permute-start(f32[4,128]{1,0:T(4,128)S(1)} %get-tuple-element.54), channel_id=1, source_target_pairs={{0,8},{8,16},{16,24},{1,9},{9,17},{17,25},{2,10},{10,18},{18,26},{... | collective-permute-start | bytes 6152 | tf_op jit(solution)/shard_map/ppermute | solution.py:223
  35.0 29.4 %collective-permute-start.4 = (f32[4,128]{1,0:T(4,128)S(1)}, f32[4,128]{1,0:T(4,128)S(1)}, u32[]{:S(2)}, u32[]{:S(2)}) collective-permute-start(f32[4,128]{1,0:T(4,128)S(1)} %get-tuple-element.53), channel_id=1, source_target_pairs={{8,0},{16,8},{24,16},{9,1},{17,9},{25,17},{10,2},{18,10},{26,18},{... | collective-permute-start | bytes 6152 | tf_op jit(solution)/shard_map/ppermute | solution.py:224
  36.3 40.3 %collective-permute-start.12 = (f32[8,30,4,128]{3,2,1,0:T(4,128)}, f32[8,30,4,128]{3,2,1,0:T(4,128)S(1)}, u32[]{:S(2)}, u32[]{:S(2)}) collective-permute-start(f32[8,30,4,128]{3,2,1,0:T(4,128)} %get-tuple-element.26), channel_id=1, source_target_pairs={{8,0},{16,8},{24,16},{9,1},{17,9},{25,17},{10,2},{18,10},{26,18},{... | collective-permute-start | bytes 1474568 | tf_op jit(solution)/shard_map/ppermute | solution.py:224
  37.6 40.3 %collective-permute-start.13 = (f32[8,30,4,128]{3,2,1,0:T(4,128)}, f32[8,30,4,128]{3,2,1,0:T(4,128)}, u32[]{:S(2)}, u32[]{:S(2)}) collective-permute-start(f32[8,30,4,128]{3,2,1,0:T(4,128)} %get-tuple-element.25), channel_id=1, source_target_pairs={{0,8},{8,16},{16,24},{1,9},{9,17},{17,25},{2,10},{10,18},{18,26},{... | collective-permute-start | bytes 1474568 | tf_op jit(solution)/shard_map/ppermute | solution.py:223
  51.2 6.7 %copy-start.2 = (f32[30,16,128]{2,1,0:T(8,128)S(1)}, f32[30,16,128]{2,1,0:T(8,128)}, u32[]{:S(2)}) copy-start(f32[30,16,128]{2,1,0:T(8,128)} %param.12) | copy-start | bytes 737284
  60.2 6.0 %collective-permute-start.7 = (f32[30,4,128]{2,1,0:T(4,128)S(1)}, f32[30,4,128]{2,1,0:T(4,128)S(1)}, u32[]{:S(2)}, u32[]{:S(2)}) collective-permute-start(f32[30,4,128]{2,1,0:T(4,128)S(1)} %get-tuple-element.42), channel_id=1, source_target_pairs={{0,8},{8,16},{16,24},{1,9},{9,17},{17,25},{2,10},{10,18},{18,26},{... | collective-permute-start | bytes 184328 | tf_op jit(solution)/shard_map/ppermute | solution.py:223
  64.3 6.3 %collective-permute-start.6 = (f32[30,4,128]{2,1,0:T(4,128)S(1)}, f32[30,4,128]{2,1,0:T(4,128)S(1)}, u32[]{:S(2)}, u32[]{:S(2)}) collective-permute-start(f32[30,4,128]{2,1,0:T(4,128)S(1)} %get-tuple-element.41), channel_id=1, source_target_pairs={{8,0},{16,8},{24,16},{9,1},{17,9},{25,17},{10,2},{18,10},{26,18},{... | collective-permute-start | bytes 184328 | tf_op jit(solution)/shard_map/ppermute | solution.py:224
  66.2 88.2 %collective-permute-start.1 = (f32[8,30,4,128]{3,2,1,0:T(4,128)}, f32[8,30,4,128]{3,2,1,0:T(4,128)S(1)}, u32[]{:S(2)}, u32[]{:S(2)}) collective-permute-start(f32[8,30,4,128]{3,2,1,0:T(4,128)} %get-tuple-element.31), channel_id=1, source_target_pairs={{0,8},{8,16},{16,24},{1,9},{9,17},{17,25},{2,10},{10,18},{18,26},{... | collective-permute-start | bytes 1474568 | tf_op jit(solution)/shard_map/ppermute | solution.py:223
  70.6 65.3 %collective-permute-start.8 = (f32[8,30,4,128]{3,2,1,0:T(4,128)}, f32[8,30,4,128]{3,2,1,0:T(4,128)S(1)}, u32[]{:S(2)}, u32[]{:S(2)}) collective-permute-start(f32[8,30,4,128]{3,2,1,0:T(4,128)} %get-tuple-element.30), channel_id=1, source_target_pairs={{8,0},{16,8},{24,16},{9,1},{17,9},{25,17},{10,2},{18,10},{26,18},{... | collective-permute-start | bytes 1474568 | tf_op jit(solution)/shard_map/ppermute | solution.py:224
  76.6 30.2 %collective-permute-start.10 = (f32[8,30,4,128]{3,2,1,0:T(4,128)}, f32[8,30,4,128]{3,2,1,0:T(4,128)S(1)}, u32[]{:S(2)}, u32[]{:S(2)}) collective-permute-start(f32[8,30,4,128]{3,2,1,0:T(4,128)} %get-tuple-element.28), channel_id=1, source_target_pairs={{8,0},{16,8},{24,16},{9,1},{17,9},{25,17},{10,2},{18,10},{26,18},{... | collective-permute-start | bytes 1474568 | tf_op jit(solution)/shard_map/ppermute | solution.py:224
  77.9 32.2 %collective-permute-start.11 = (f32[8,30,4,128]{3,2,1,0:T(4,128)}, f32[8,30,4,128]{3,2,1,0:T(4,128)S(1)}, u32[]{:S(2)}, u32[]{:S(2)}) collective-permute-start(f32[8,30,4,128]{3,2,1,0:T(4,128)} %get-tuple-element.27), channel_id=1, source_target_pairs={{0,8},{8,16},{16,24},{1,9},{9,17},{17,25},{2,10},{10,18},{18,26},{... | collective-permute-start | bytes 1474568 | tf_op jit(solution)/shard_map/ppermute | solution.py:223
  87.8 19.0 %copy-start.3 = (f32[8,30,4,128]{3,2,1,0:T(4,128)S(1)}, f32[8,30,4,128]{3,2,1,0:T(4,128)}, u32[]{:S(2)}) copy-start(f32[8,30,4,128]{3,2,1,0:T(4,128)} %get-tuple-element.29) | copy-start | bytes 1474564
  106.8 30.5 %collective-permute-start.9 = (f32[8,30,4,128]{3,2,1,0:T(4,128)S(1)}, f32[8,30,4,128]{3,2,1,0:T(4,128)S(1)}, u32[]{:S(2)}, u32[]{:S(2)}) collective-permute-start(f32[8,30,4,128]{3,2,1,0:T(4,128)S(1)} %copy-done.3), channel_id=1, source_target_pairs={{0,8},{8,16},{16,24},{1,9},{9,17},{17,25},{2,10},{10,18},{18,26},{... | collective-permute-start | bytes 1474568 | tf_op jit(solution)/shard_map/ppermute | solution.py:223
  110.1 68.5 %collective-permute-start.17 = (f32[1,128]{1,0:T(1,128)S(1)}, f32[1,128]{1,0:T(1,128)S(1)}, u32[]{:S(2)}, u32[]{:S(2)}) collective-permute-start(f32[1,128]{1,0:T(1,128)S(1)} %get-tuple-element.52), channel_id=1, source_target_pairs={{0,8},{8,16},{16,24},{1,9},{9,17},{17,25},{2,10},{10,18},{18,26},{... | collective-permute-start | bytes 1544 | tf_op jit(solution)/shard_map/ppermute | solution.py:223
  135.9 42.7 %collective-permute-start.16 = (f32[1,128]{1,0:T(1,128)S(1)}, f32[1,128]{1,0:T(1,128)S(1)}, u32[]{:S(2)}, u32[]{:S(2)}) collective-permute-start(f32[1,128]{1,0:T(1,128)S(1)} %get-tuple-element.51), channel_id=1, source_target_pairs={{8,0},{16,8},{24,16},{9,1},{17,9},{25,17},{10,2},{18,10},{26,18},{... | collective-permute-start | bytes 1544 | tf_op jit(solution)/shard_map/ppermute | solution.py:224
  154.4 29.8 %copy-start.1 = (f32[32,16,128]{2,1,0:T(8,128)S(1)}, f32[32,16,128]{2,1,0:T(8,128)}, u32[]{:S(2)}) copy-start(f32[32,16,128]{2,1,0:T(8,128)} %param.15) | copy-start | bytes 786436
  171.5 7.4 %collective-permute-start.15 = (f32[32,2,1,128]{3,2,1,0:T(1,128)S(1)}, f32[32,2,1,128]{3,2,1,0:T(1,128)S(1)}, u32[]{:S(2)}, u32[]{:S(2)}) collective-permute-start(f32[32,2,1,128]{3,2,1,0:T(1,128)S(1)} %get-tuple-element.38), channel_id=1, source_target_pairs={{0,8},{8,16},{16,24},{1,9},{9,17},{17,25},{2,10},{10,18},{18,26},{... | collective-permute-start | bytes 98312 | tf_op jit(solution)/shard_map/ppermute | solution.py:223
  177.3 6.7 %collective-permute-start.14 = (f32[32,2,1,128]{3,2,1,0:T(1,128)S(1)}, f32[32,2,1,128]{3,2,1,0:T(1,128)S(1)}, u32[]{:S(2)}, u32[]{:S(2)}) collective-permute-start(f32[32,2,1,128]{3,2,1,0:T(1,128)S(1)} %get-tuple-element.37), channel_id=1, source_target_pairs={{8,0},{16,8},{24,16},{9,1},{17,9},{25,17},{10,2},{18,10},{26,18},{... | collective-permute-start | bytes 98312 | tf_op jit(solution)/shard_map/ppermute | solution.py:224
  (5 other events, 26.1 us)
Sparse Core Ops, SparseCore 0:
  23.5 37.8 all-gather.3

commit v2 on v1

--- a/solution.py
+++ b/solution.py
@@ -99,34 +99,141 @@
             out_ref[g] = x_ref[g, :, :own, :]
 
 
-def score_kernel(tq_ref, ext_ref, land_ref, b_hi_ref, b_lo_ref, head_ref, out_ref):
+def peers(axis, send):
+    size = lax.axis_size(axis)
+    me = lax.axis_index(axis)
+    for d in range(1, size):
+        send(lax.rem(me + d, size), d)
+
+
+def exchange(axis, mine_ref, slots_ref, send_sem, recv_sem):
+    me = lax.axis_index(axis)
+
+    def copy(other, slot, d):
+        return pltpu.make_async_remote_copy(
+            src_ref=mine_ref,
+            dst_ref=slots_ref.at[slot],
+            send_sem=send_sem.at[d],
+            recv_sem=recv_sem.at[slot],
+            device_id={axis: other},
+            device_id_type=pl.DeviceIdType.MESH,
+        )
+
+    peers(axis, lambda other, d: copy(other, me, d).start())
+    slots_ref[me] = mine_ref[...]
+    peers(axis, lambda other, d: copy(other, other, d).wait_recv())
+    peers(axis, lambda other, d: copy(other, me, d).wait_send())
+
+
+def greet():
+    barrier = pltpu.get_barrier_semaphore()
+    for axis in ("lat", "grp"):
+        peers(
+            axis,
+            lambda other, d: pl.semaphore_signal(
+                barrier, inc=1, device_id={axis: other}, device_id_type=pl.DeviceIdType.MESH
+            ),
+        )
+    pl.semaphore_wait(barrier, lax.axis_size("lat") + lax.axis_size("grp") - 2)
+
+
+def finish_kernel(
+    tq_ref, land_ref, b_hi_ref, b_lo_ref, head_ref, out_ref,
+    first_ref, last_ref, below_ref, above_ref, part_ref, mine_ref, lat_slots, sum_ref, grp_slots,
+    edge_send, edge_recv, lat_send, lat_recv, grp_send, grp_recv,
+):
     members, _, own, lon = tq_ref.shape
+    me, size = lax.axis_index("lat"), lax.axis_size("lat")
+    for m in range(members):
+        for k in range(2):
+            at = 2 * m + k
+            first_ref[at : at + 1, :] = tq_ref[m, k, 0:1, :]
+            last_ref[at : at + 1, :] = tq_ref[m, k, own - 1 : own, :]
+    greet()
+
+    def edge(way, other):
+        return pltpu.make_async_remote_copy(
+            src_ref=(first_ref, last_ref)[way],
+            dst_ref=(below_ref, above_ref)[way],
+            send_sem=edge_send.at[way],
+            recv_sem=edge_recv.at[way],
+            device_id={"lat": other},
+            device_id_type=pl.DeviceIdType.MESH,
+        )
+
+    @pl.when(me > 0)
+    def _():
+        edge(0, me - 1).start()
+
+    @pl.when(me < size - 1)
+    def _():
+        edge(1, me + 1).start()
+
+    @pl.when(me > 0)
+    def _():
+        edge(1, me - 1).wait_recv()
+        edge(0, me - 1).wait_send()
+
+    @pl.when(me < size - 1)
+    def _():
+        edge(0, me + 1).wait_recv()
+        edge(1, me + 1).wait_send()
+
+    @pl.when(me == 0)
+    def _():
+        above_ref[...] = jnp.zeros_like(above_ref)
+
+    @pl.when(me == size - 1)
+    def _():
+        below_ref[...] = jnp.zeros_like(below_ref)
+
     land = land_ref[...]
-    depth = b_hi_ref.shape[1]
-    pad = depth - 9 * (own + SUB)
-    highs, lows = [], []
-    for g in range(members):
-        t = jnp.concatenate([tq_ref[g, 0], ext_ref[g, 0]], axis=0)
-        q = jnp.concatenate([tq_ref[g, 1], ext_ref[g, 1]], axis=0)
-        rows = []
-        for value in (t * land, q, t * (1.0 - land)):
-            rows += [pltpu.roll(value, 1, 1), value, pltpu.roll(value, lon - 1, 1)]
-        if pad:
-            rows.append(jnp.zeros((pad, lon), F32))
-        hi, lo = split_hi_lo(jnp.concatenate(rows, axis=0))
-        highs.append(hi)
-        lows.append(lo)
-    for g in range(0, members, 2):
+    pad = b_hi_ref.shape[1] - 9 * (own + SUB)
+    place = lax.broadcasted_iota(jnp.int32, (SUB, lon), 0)
+
+    def pair(i, carry):
+        highs, lows = [], []
+        for g in range(2):
+            values = []
+            for k in range(2):
+                at = 4 * i + 2 * g + k
+                ext = jnp.where(
+                    place == 0,
+                    below_ref[pl.ds(at, 1), :],
+                    jnp.where(place == SUB - 1, above_ref[pl.ds(at, 1), :], 0.0),
+                )
+                values.append(jnp.concatenate([tq_ref[2 * i + g, k], ext], axis=0))
+            t, q = values
+            rows = []
+            for value in (t * land, q, t * (1.0 - land)):
+                rows += [pltpu.roll(value, 1, 1), value, pltpu.roll(value, lon - 1, 1)]
+            if pad:
+                rows.append(jnp.zeros((pad, lon), F32))
+            hi, lo = split_hi_lo(jnp.concatenate(rows, axis=0))
+            highs.append(hi)
+            lows.append(lo)
         hidden = dot3(
-            b_hi_ref[...],
-            b_lo_ref[...],
-            jnp.concatenate(highs[g : g + 2], axis=1),
-            jnp.concatenate(lows[g : g + 2], axis=1),
+            b_hi_ref[...], b_lo_ref[...], jnp.concatenate(highs, axis=1), jnp.concatenate(lows, axis=1)
         )
         hidden = jnp.maximum(hidden, 0.0)
-        for k in range(2):
-            terms = hidden[:, k * lon : (k + 1) * lon] * head_ref[...]
-            out_ref[g + k : g + k + 1, :] = jnp.sum(terms, axis=0, keepdims=True)
+        for g in range(2):
+            terms = hidden[:, g * lon : (g + 1) * lon] * head_ref[...]
+            part_ref[pl.ds(2 * i + g, 1), :] = jnp.sum(terms, axis=0, keepdims=True)
+        return carry
+
+    lax.fori_loop(0, members // 2, pair, 0)
+    total = jnp.sum(part_ref[...], axis=1, keepdims=True)
+    row = lax.broadcasted_iota(jnp.int32, (members, lon), 0)
+    col = lax.broadcasted_iota(jnp.int32, (members, lon), 1)
+    flat = jnp.sum(jnp.where(row == col, total, 0.0), axis=0, keepdims=True)
+    mine_ref[...] = jnp.broadcast_to(flat, mine_ref.shape)
+    exchange("lat", mine_ref, lat_slots, lat_send, lat_recv)
+    score = lat_slots[0]
+    for k in range(1, size):
+        score = score + lat_slots[k]
+    sum_ref[...] = score
+    exchange("grp", sum_ref, grp_slots, grp_send, grp_recv)
+    out_ref[...] = grp_slots[...]
 
 
 def params():
@@ -195,25 +302,35 @@
     )(*ins)
 
 
-def run_scores(tq, ext, land, b_hi, b_lo, head):
+def run_finish(tq, land, b_hi, b_lo, head):
     members, _, own, lon = tq.shape
-    group = 8
+    lat, grp = lax.axis_size("lat"), lax.axis_size("grp")
+    edge = pltpu.VMEM((2 * members, lon), F32)
+    tile = pltpu.VMEM((SUB, lon), F32)
     return pl.pallas_call(
-        score_kernel,
-        out_shape=jax.ShapeDtypeStruct((members, lon), F32),
-        in_specs=[
-            pl.BlockSpec((group, 2, own, lon), lambda i: (i, 0, 0, 0)),
-            pl.BlockSpec((group, 2, SUB, lon), lambda i: (i, 0, 0, 0)),
-            full_spec(land),
-            full_spec(b_hi),
-            full_spec(b_lo),
-            full_spec(head),
+        finish_kernel,
+        out_shape=jax.ShapeDtypeStruct((grp, SUB, lon), F32),
+        in_specs=[pl.BlockSpec(memory_space=pltpu.VMEM)] * 5,
+        out_specs=pl.BlockSpec(memory_space=pltpu.VMEM),
+        scratch_shapes=[
+            edge, edge, edge, edge,
+            pltpu.VMEM((members, lon), F32),
+            tile,
+            pltpu.VMEM((lat, SUB, lon), F32),
+            tile,
+            pltpu.VMEM((grp, SUB, lon), F32),
+            pltpu.SemaphoreType.DMA((2,)),
+            pltpu.SemaphoreType.DMA((2,)),
+            pltpu.SemaphoreType.DMA((lat,)),
+            pltpu.SemaphoreType.DMA((lat,)),
+            pltpu.SemaphoreType.DMA((grp,)),
+            pltpu.SemaphoreType.DMA((grp,)),
         ],
-        out_specs=pl.BlockSpec((group, lon), lambda i: (i, 0)),
-        grid=(members // group,),
-        compiler_params=params(),
-        name="score_terms",
-    )(tq, ext, land, b_hi, b_lo, head)
+        compiler_params=pltpu.CompilerParams(
+            collective_id=0, has_side_effects=True, vmem_limit_bytes=40 * 2**20
+        ),
+        name="finish",
+    )(tq, land, b_hi, b_lo, head)
 
 
 def halos(value, dim, width, axis="lat"):
@@ -249,13 +366,14 @@
     killed = (local_source != offset + jnp.arange(members, dtype=jnp.int32)).astype(jnp.int32)
     donor_group = jnp.max(jnp.where(killed > 0, local_source // members, 0))
 
+    land = land_mask.astype(F32)
     hot = lax.dynamic_index_in_dim(fields, jnp.argmax(local_counts), 0, keepdims=False)
-    hot_all = jnp.concatenate([hot, *halos(hot, 1, STEPS)], axis=1)
+    stack = jnp.concatenate([hot, heating, diffusion[None], land[None]], axis=0)
+    stack_all = jnp.concatenate([stack, *halos(stack, 1, STEPS)], axis=1)
+    hot_all, heat_all = stack_all[:levels], stack_all[levels : 2 * levels]
+    diff_all, land_all = stack_all[2 * levels], stack_all[2 * levels + 1]
     gathered = lax.all_gather(hot_all, "grp", axis=0)
     donor_all = lax.dynamic_index_in_dim(gathered, donor_group, 0, keepdims=True)
-
-    diff_all = jnp.concatenate([diffusion, *halos(diffusion, 0, STEPS)], axis=0)
-    heat_all = jnp.concatenate([heating, *halos(heating, 1, STEPS)], axis=1)
     eye = jnp.eye(SUB, dtype=F32)
     wide = (mixing[:, None, :, None] * eye[None, :, None, :]).reshape(levels * SUB, levels * SUB)
     consts = (diff_all, heat_all, *split_constant(wide))
@@ -275,16 +393,9 @@
         parts.append(tq)
     tq = jnp.concatenate(parts, axis=0)
 
-    land = land_mask.astype(F32)
-    land_below, land_above = halos(land, 0, 1)
-    land_all = jnp.concatenate([land, land_below, jnp.zeros((SUB - 2, lon), F32), land_above], axis=0)
-    tq_below, tq_above = halos(tq, 2, 1)
-    ext = jnp.concatenate([tq_below, jnp.zeros((members, 2, SUB - 2, lon), F32), tq_above], axis=2)
     b_hi, b_lo = split_constant(conv_matrix(conv_weight, own))
-    partial = run_scores(tq, ext, land_all, b_hi, b_lo, head_weight.reshape(-1, lon))
-    partial = jnp.sum(partial, axis=1)
-    everything = lax.all_gather(partial, ("lat", "grp"), axis=0)
-    all_scores = everything.reshape(lax.axis_size("lat"), total_members).sum(0)
+    table = run_finish(tq, land_all, b_hi, b_lo, head_weight.reshape(-1, lon))
+    all_scores = table[:, 0, :members].reshape(total_members)
     scores = lax.dynamic_slice_in_dim(all_scores, offset, members)
     weights = jnp.exp(all_scores)
     weights = weights / jnp.mean(weights)

time: 240 us -> 203 us (0.85)
  blocking collectives: 40.5 us -> 0 us
  starting transfers between devices: 61.2 us -> 38.8 us
  Pallas kernels: 75.7 us -> 93 us
  waiting for transfers between devices: 12.4 us -> 16.1 us
  other arithmetic: 9.79 us -> 13.2 us
    unnamed x1 -> x0, blocking collectives: 40.5 us -> none
    ppermute x9 -> x5, starting transfers between devices: 49.5 us -> 32.4 us  [halos(): lax.ppermute(lax.slice_in_dim(value, length - width, length, axis=dim), a...]
    pallas_call x1, Pallas kernels: 4.49 us -> 21.6 us  [run_finish(): pl.pallas_call(finish_kernel, out_shape=jax.ShapeDtypeStruct((grp, SUB, l...]
    ppermute x9 -> x5, starting transfers between devices: 11.6 us -> 6.44 us  [halos(): lax.ppermute(lax.slice_in_dim(value, 0, width, axis=dim), axis, down)]
    ppermute x9 -> x5, waiting for transfers between devices: 11.1 us -> 14.7 us  [halos(): lax.ppermute(lax.slice_in_dim(value, 0, width, axis=dim), axis, down)]
  transfers between devices with their start and end apart: 19 -> 11, of which waited for: 7 -> 3; matrix products, arithmetic and copies ran while one was open for 9% -> 12% of each run, Pallas kernels for 30% -> 27%
where the time goes in v2:
time: 203 us; the launch traced here: 202 us
  Pallas kernels  93 us (46%)
  starting transfers between devices  38.8 us (19%)
  local copies, waits for them, and re-layouts  22 us (11%)
  between operations  18.9 us (9%)
  waiting for transfers between devices  16.1 us (8%)
  other arithmetic  13.2 us (7%)
    pallas_call x4, Pallas kernels, run_chunk(): pl.pallas_call(functools.partial(chunk_kernel, first), out_shape=(jax.Sha...  68.8 us
    ppermute x5, starting transfers between devices, halos(): lax.ppermute(lax.slice_in_dim(value, length - width, length, axis=dim), a...  32.4 us
    pallas_call x1, Pallas kernels, run_finish(): pl.pallas_call(finish_kernel, out_shape=jax.ShapeDtypeStruct((grp, SUB, l...  21.6 us
    ppermute x5, waiting for transfers between devices, halos(): lax.ppermute(lax.slice_in_dim(value, 0, width, axis=dim), axis, down)  14.7 us
    ppermute x5, starting transfers between devices, halos(): lax.ppermute(lax.slice_in_dim(value, 0, width, axis=dim), axis, down)  6.44 us
    slice x1, local copies, waits for them, and re-layouts, halos(): lax.slice_in_dim(value, length - width, length, axis=dim)  5.42 us
    add x1, local copies, waits for them, and re-layouts, conv_matrix(): matrix = (parts[0] + parts[1] + parts[2]).reshape(channels * own, 9 * rows)  4.07 us
  transfers between devices with their start and end apart: 11, of which 3 were waited for; matrix products, arithmetic and copies ran while one was open for 12% of the time, Pallas kernels for 27%

profile of v2, /device:TPU:0, one launch (start us, length us, event | category | flops | bytes accessed | tf_op | source)
XLA Modules:
  0.0 202.0 jit_solution(7051128517923359435)
XLA Ops:
  7.2 1.4 iota_reduce_fusion
  13.3 4.8 %collective-permute-start.3 = (f32[62,4,128]{2,1,0:T(4,128)S(1)}, f32[62,4,128]{2,1,0:T(4,128)S(1)}, u32[]{:S(2)}, u32[]{:S(2)}) collective-permute-start(f32[62,4,128]{2,1,0:T(4,128)S(1)} %get-tuple-element.44), channel_id=1, source_target_pairs={{0,8},{8,16},{16,24},{1,9},{9,17},{17,25},{2,10},{10,18},{18,26},{... | collective-permute-start | bytes 380936 | tf_op jit(solution)/shard_map/ppermute | solution.py:340
  18.1 1.3 collective-permute-start.2
  19.4 1.3 collective-permute-done.3
  20.8 4.7 %collective-permute-done.2 = f32[62,4,128]{2,1,0:T(4,128)S(1)} collective-permute-done((f32[62,4,128]{2,1,0:T(4,128)S(1)}, f32[62,4,128]{2,1,0:T(4,128)S(1)}, u32[]{:S(2)}, u32[]{:S(2)}) %collective-permute-start.2) | collective-permute-done | bytes 127008 | tf_op jit(solution)/shard_map/ppermute | solution.py:341
  28.0 5.4 %fusion.8 = (f32[8,30,4,128]{3,2,1,0:T(4,128)}, f32[8,30,4,128]{3,2,1,0:T(4,128)}, f32[8,30,4,128]{3,2,1,0:T(4,128)}, f32[8,30,4,128]{3,2,1,0:T(4,128)}, f32[8,3...) fusion(f32[32,30,16,128]{3,2,1,0:T(8,128)} %fields_ref.7), kind=kLoop, calls=%fused_computation.50 | loop fusion | bytes 7864320 | tf_op jit(solution)/shard_map/slice | solution.py:340
  34.7 1.3 collective-permute-start.6
  36.0 5.2 %collective-permute-start.7 = (f32[8,30,4,128]{3,2,1,0:T(4,128)}, f32[8,30,4,128]{3,2,1,0:T(4,128)S(1)}, u32[]{:S(2)}, u32[]{:S(2)}) collective-permute-start(f32[8,30,4,128]{3,2,1,0:T(4,128)} %get-tuple-element.29), channel_id=1, source_target_pairs={{0,8},{8,16},{16,24},{1,9},{9,17},{17,25},{2,10},{10,18},{18,26},{... | collective-permute-start | bytes 1474568 | tf_op jit(solution)/shard_map/ppermute | solution.py:340
  41.2 1.3 collective-permute-start.8
  42.5 6.2 %collective-permute-start.9 = (f32[8,30,4,128]{3,2,1,0:T(4,128)}, f32[8,30,4,128]{3,2,1,0:T(4,128)}, u32[]{:S(2)}, u32[]{:S(2)}) collective-permute-start(f32[8,30,4,128]{3,2,1,0:T(4,128)} %get-tuple-element.27), channel_id=1, source_target_pairs={{0,8},{8,16},{16,24},{1,9},{9,17},{17,25},{2,10},{10,18},{18,26},{... | collective-permute-start | bytes 1474568 | tf_op jit(solution)/shard_map/ppermute | solution.py:340
  48.8 2.5 %broadcast_multiply_fusion = f32[30,8,30,8]{3,2,1,0:T(8,128)} fusion(f32[8,8]{1,0:T(8,128)S(1)} %fusion.3, f32[30,30]{1,0:T(8,128)S(1)} %copy-done.5), kind=kLoop, calls=%fused_computation.1 | loop fusion | flops 57600 | bytes 234256 | tf_op jit(solution)/shard_map/mul | solution.py:378
  51.3 3.7 %mul.97 = f32[240,240]{1,0:T(8,128)S(1)} reshape(f32[30,8,30,8]{3,2,1,0:T(8,128)} %broadcast_multiply_fusion) | data formatting | bytes 460800 | tf_op jit(solution)/shard_map/mul | solution.py:378
  56.3 2.5 %multiply_add_fusion = f32[32,16,3,3,24]{4,3,2,1,0:T(4,128)} fusion(f32[16,24]{1,0:T(8,128)S(1)} %get-tuple-element.48, f32[32,3,3]{2,1,0:T(4,128)S(1)} %copy.26, f32[16,24]{1,0:T(8,128)S(1)} %get-tuple-element.49, f32[32,3,3]{2,1,0:T(4,128)S(1)} %copy.25, f32[16,24]{1,0:T(8,128)S(1)} %get-tuple-element.47, f32[32,3,3]{2,1,0:T(4,128)S(1)} %copy.24), kind=kLoop, calls=%fused_computation | loop fusion | flops 552960 | bytes 450432 | tf_op jit(solution)/shard_map/add | solution.py:354
  60.2 4.1 %add.96 = f32[512,216]{1,0:T(8,128)} reshape(f32[32,16,3,3,24]{4,3,2,1,0:T(4,128)} %multiply_add_fusion) | data formatting | bytes 884736 | tf_op jit(solution)/shard_map/add | solution.py:354
  68.7 2.5 %donor_steps.1.donor_ref = f32[1,30,16,128]{3,2,1,0:T(8,128)S(1)} custom-call(f32[1,30,16,128]{3,2,1,0:T(8,128)S(1)} %constant_dynamic-slice_fusion.1.fields_ref, f32[1,30,4,128]{3,2,1,0:T(4,128)S(1)} %get-tuple-element.36.below_ref, f32[1,30,4,128]{3,2,1,0:T(4,128)S(1)} %get-tuple-element.35.above_ref, f32[24,128]{1,0:T(8,128)S(1)} %get-tuple-element.38.diff_ref, ...), custom_call_target="tpu_custom_call" | custom-call | tf_op jit(solution)/shard_map/donor_steps/pallas_call | solution.py:260
  71.3 10.0 %collective-permute-done.8.below_ref = f32[8,30,4,128]{3,2,1,0:T(4,128)S(1)} collective-permute-done((f32[8,30,4,128]{3,2,1,0:T(4,128)}, f32[8,30,4,128]{3,2,1,0:T(4,128)S(1)}, u32[]{:S(2)}, u32[]{:S(2)}) %collective-permute-start.8) | collective-permute-done | bytes 491552 | tf_op jit(solution)/shard_map/ppermute | solution.py:341
  82.6 10.8 %collective-permute-start.5 = (f32[8,30,4,128]{3,2,1,0:T(4,128)}, f32[8,30,4,128]{3,2,1,0:T(4,128)S(1)}, u32[]{:S(2)}, u32[]{:S(2)}) collective-permute-start(f32[8,30,4,128]{3,2,1,0:T(4,128)} %get-tuple-element.31), channel_id=1, source_target_pairs={{0,8},{8,16},{16,24},{1,9},{9,17},{17,25},{2,10},{10,18},{18,26},{... | collective-permute-start | bytes 1474568 | tf_op jit(solution)/shard_map/ppermute | solution.py:340
  93.4 3.2 %copy-done = f32[32,30,16,128]{3,2,1,0:T(8,128)S(1)} copy-done((f32[32,30,16,128]{3,2,1,0:T(8,128)S(1)}, f32[32,30,16,128]{3,2,1,0:T(8,128)}, u32[]{:S(2)}) %copy-start) | copy-done | bytes 7864344
  96.6 17.5 %chunk_steps.4 = (f32[32,30,16,128]{3,2,1,0:T(8,128)}, f32[8,2,16,128]{3,2,1,0:T(8,128)S(1)}) custom-call(s32[32]{0:T(128)S(1)} %compare_convert_fusion.killed_ref, f32[32,30,16,128]{3,2,1,0:T(8,128)S(1)} %copy-done, f32[8,30,4,128]{3,2,1,0:T(4,128)S(1)} %collective-permute-done.8.below_ref, f32[8,30,4,128]{3,2,1,0:T(4,128)} %collective-permute-done.9.above_ref, ...), custom_call_target="tpu_custom_call" | custom-call | flops 4246732800 | bytes 3932160 | tf_op jit(solution)/shard_map/chunk_steps/pallas_call | solution.py:288
  114.1 5.3 %collective-permute-start.1 = (f32[8,30,4,128]{3,2,1,0:T(4,128)S(1)}, f32[8,30,4,128]{3,2,1,0:T(4,128)S(1)}, u32[]{:S(2)}, u32[]{:S(2)}) collective-permute-start(f32[8,30,4,128]{3,2,1,0:T(4,128)S(1)} %copy-done.3), channel_id=1, source_target_pairs={{0,8},{8,16},{16,24},{1,9},{9,17},{17,25},{2,10},{10,18},{18,26},{... | collective-permute-start | bytes 1474568 | tf_op jit(solution)/shard_map/ppermute | solution.py:340
  119.4 17.1 %chunk_steps.5 = (f32[32,30,16,128]{3,2,1,0:T(8,128)}, f32[8,2,16,128]{3,2,1,0:T(8,128)S(1)}) custom-call(s32[32]{0:T(128)S(1)} %compare_convert_fusion.killed_ref, f32[32,30,16,128]{3,2,1,0:T(8,128)S(1)} %copy-done, f32[8,30,4,128]{3,2,1,0:T(4,128)S(1)} %collective-permute-done.6.below_ref, ...), custom_call_target="tpu_custom_call", output_to_operand_aliasing={{0}: (9, {})} | custom-call | flops 4246732800 | bytes 3932160 | tf_op jit(solution)/shard_map/chunk_steps/pallas_call | solution.py:288
  136.6 17.1 %chunk_steps.6 = (f32[32,30,16,128]{3,2,1,0:T(8,128)}, f32[8,2,16,128]{3,2,1,0:T(8,128)S(1)}) custom-call(s32[32]{0:T(128)S(1)} %compare_convert_fusion.killed_ref, f32[32,30,16,128]{3,2,1,0:T(8,128)S(1)} %copy-done, f32[8,30,4,128]{3,2,1,0:T(4,128)S(1)} %collective-permute-done.4.below_ref, ...), custom_call_target="tpu_custom_call", output_to_operand_aliasing={{0}: (9, {})} | custom-call | flops 4246732800 | bytes 3932160 | tf_op jit(solution)/shard_map/chunk_steps/pallas_call | solution.py:288
  153.6 17.1 %chunk_steps.7 = (f32[32,30,16,128]{3,2,1,0:T(8,128)}, f32[8,2,16,128]{3,2,1,0:T(8,128)S(1)}) custom-call(s32[32]{0:T(128)S(1)} %compare_convert_fusion.killed_ref, f32[32,30,16,128]{3,2,1,0:T(8,128)S(1)} %copy-done, f32[8,30,4,128]{3,2,1,0:T(4,128)S(1)} %collective-permute-done.below_ref, ...), custom_call_target="tpu_custom_call", output_to_operand_aliasing={{0}: (9, {})} | custom-call | flops 4246732800 | bytes 3932160 | tf_op jit(solution)/shard_map/chunk_steps/pallas_call | solution.py:288
  170.8 21.6 %finish.1 = f32[8,8,128]{2,1,0:T(8,128)S(1)} custom-call(f32[32,2,16,128]{3,2,1,0:T(8,128)S(1)} %pad_maximum_fusion.1.tq_ref, f32[24,128]{1,0:T(8,128)S(1)} %get-tuple-element.37.land_ref, bf16[512,224]{1,0:T(8,128)(2,1)S(1)} %get-tuple-element.42.b_hi_ref, bf16[512,224]{1,0:T(8,128)(2,1)S(1)} %get-tuple-element.41.b_lo_ref, f32[512,128]{1,0:T(8,128)S(1)} %bitcast.25), custom_call_target="tpu_custom_call" | custom-call | tf_op jit(solution)/shard_map/finish/pallas_call | solution.py:310
  (59 shorter events, 15.0 us)
Async XLA Ops:
  7.2 59.6 %all-gather.3.cloned.1.call-start = ((), (), s32[]{:S(2)}) async-start(), calls=%async_computation | async-start | bytes 3317760 | tf_op jit(solution)/shard_map/all_gather | solution.py:375
  13.3 7.5 %collective-permute-start.3 = (f32[62,4,128]{2,1,0:T(4,128)S(1)}, f32[62,4,128]{2,1,0:T(4,128)S(1)}, u32[]{:S(2)}, u32[]{:S(2)}) collective-permute-start(f32[62,4,128]{2,1,0:T(4,128)S(1)} %get-tuple-element.44), channel_id=1, source_target_pairs={{0,8},{8,16},{16,24},{1,9},{9,17},{17,25},{2,10},{10,18},{18,26},{... | collective-permute-start | bytes 380936 | tf_op jit(solution)/shard_map/ppermute | solution.py:340
  18.1 7.3 %collective-permute-start.2 = (f32[62,4,128]{2,1,0:T(4,128)S(1)}, f32[62,4,128]{2,1,0:T(4,128)S(1)}, u32[]{:S(2)}, u32[]{:S(2)}) collective-permute-start(f32[62,4,128]{2,1,0:T(4,128)S(1)} %get-tuple-element.43), channel_id=1, source_target_pairs={{8,0},{16,8},{24,16},{9,1},{17,9},{25,17},{10,2},{18,10},{26,18},{... | collective-permute-start | bytes 380936 | tf_op jit(solution)/shard_map/ppermute | solution.py:341
  25.5 0.6 copy-start.2
  28.0 20.8 %copy-start.5 = (f32[30,30]{1,0:T(8,128)S(1)}, f32[30,30]{1,0:T(8,128)}, u32[]{:S(2)}) copy-start(f32[30,30]{1,0:T(8,128)} %param.11) | copy-start | bytes 10804
  33.4 120.2 %collective-permute-start = (f32[8,30,4,128]{3,2,1,0:T(4,128)}, f32[8,30,4,128]{3,2,1,0:T(4,128)S(1)}, u32[]{:S(2)}, u32[]{:S(2)}) collective-permute-start(f32[8,30,4,128]{3,2,1,0:T(4,128)} %get-tuple-element.34), channel_id=1, source_target_pairs={{8,0},{16,8},{24,16},{9,1},{17,9},{25,17},{10,2},{18,10},{26,18},{... | collective-permute-start | bytes 1474568 | tf_op jit(solution)/shard_map/ppermute | solution.py:341
  34.7 79.4 %collective-permute-start.6 = (f32[8,30,4,128]{3,2,1,0:T(4,128)}, f32[8,30,4,128]{3,2,1,0:T(4,128)S(1)}, u32[]{:S(2)}, u32[]{:S(2)}) collective-permute-start(f32[8,30,4,128]{3,2,1,0:T(4,128)} %get-tuple-element.30), channel_id=1, source_target_pairs={{8,0},{16,8},{24,16},{9,1},{17,9},{25,17},{10,2},{18,10},{26,18},{... | collective-permute-start | bytes 1474568 | tf_op jit(solution)/shard_map/ppermute | solution.py:341
  36.0 83.4 %collective-permute-start.7 = (f32[8,30,4,128]{3,2,1,0:T(4,128)}, f32[8,30,4,128]{3,2,1,0:T(4,128)S(1)}, u32[]{:S(2)}, u32[]{:S(2)}) collective-permute-start(f32[8,30,4,128]{3,2,1,0:T(4,128)} %get-tuple-element.29), channel_id=1, source_target_pairs={{0,8},{8,16},{16,24},{1,9},{9,17},{17,25},{2,10},{10,18},{18,26},{... | collective-permute-start | bytes 1474568 | tf_op jit(solution)/shard_map/ppermute | solution.py:340
  41.2 40.0 %collective-permute-start.8 = (f32[8,30,4,128]{3,2,1,0:T(4,128)}, f32[8,30,4,128]{3,2,1,0:T(4,128)S(1)}, u32[]{:S(2)}, u32[]{:S(2)}) collective-permute-start(f32[8,30,4,128]{3,2,1,0:T(4,128)} %get-tuple-element.28), channel_id=1, source_target_pairs={{8,0},{16,8},{24,16},{9,1},{17,9},{25,17},{10,2},{18,10},{26,18},{... | collective-permute-start | bytes 1474568 | tf_op jit(solution)/shard_map/ppermute | solution.py:341
  42.5 40.0 %collective-permute-start.9 = (f32[8,30,4,128]{3,2,1,0:T(4,128)}, f32[8,30,4,128]{3,2,1,0:T(4,128)}, u32[]{:S(2)}, u32[]{:S(2)}) collective-permute-start(f32[8,30,4,128]{3,2,1,0:T(4,128)} %get-tuple-element.27), channel_id=1, source_target_pairs={{0,8},{8,16},{16,24},{1,9},{9,17},{17,25},{2,10},{10,18},{18,26},{... | collective-permute-start | bytes 1474568 | tf_op jit(solution)/shard_map/ppermute | solution.py:340
  48.8 6.2 %copy-start.6 = (f32[32,27]{1,0:T(8,128)S(1)}, f32[32,27]{1,0:T(8,128)}, u32[]{:S(2)}) copy-start(f32[32,27]{1,0:T(8,128)} %param.14) | copy-start | bytes 10372
  51.3 4.2 %copy-start.8 = (s32[256]{0:T(256)S(1)}, s32[256]{0:T(256)}, u32[]{:S(2)}) copy-start(s32[256]{0:T(256)} %param.17) | copy-start | bytes 3076
  55.0 3.9 %copy-start.7 = (s32[256]{0:T(256)S(1)}, s32[256]{0:T(256)}, u32[]{:S(2)}) copy-start(s32[256]{0:T(256)} %param.16) | copy-start | bytes 3076
  58.8 7.2 %copy-start.4 = (f32[16,128]{1,0:T(8,128)S(1)}, f32[16,128]{1,0:T(8,128)}, u32[]{:S(2)}) copy-start(f32[16,128]{1,0:T(8,128)} %param.10) | copy-start | bytes 24580
  81.3 55.3 %collective-permute-start.4 = (f32[8,30,4,128]{3,2,1,0:T(4,128)}, f32[8,30,4,128]{3,2,1,0:T(4,128)S(1)}, u32[]{:S(2)}, u32[]{:S(2)}) collective-permute-start(f32[8,30,4,128]{3,2,1,0:T(4,128)} %get-tuple-element.32), channel_id=1, source_target_pairs={{8,0},{16,8},{24,16},{9,1},{17,9},{25,17},{10,2},{18,10},{26,18},{... | collective-permute-start | bytes 1474568 | tf_op jit(solution)/shard_map/ppermute | solution.py:341
  82.6 54.0 %collective-permute-start.5 = (f32[8,30,4,128]{3,2,1,0:T(4,128)}, f32[8,30,4,128]{3,2,1,0:T(4,128)S(1)}, u32[]{:S(2)}, u32[]{:S(2)}) collective-permute-start(f32[8,30,4,128]{3,2,1,0:T(4,128)} %get-tuple-element.31), channel_id=1, source_target_pairs={{0,8},{8,16},{16,24},{1,9},{9,17},{17,25},{2,10},{10,18},{18,26},{... | collective-permute-start | bytes 1474568 | tf_op jit(solution)/shard_map/ppermute | solution.py:340
  93.4 3.2 %copy-start = (f32[32,30,16,128]{3,2,1,0:T(8,128)S(1)}, f32[32,30,16,128]{3,2,1,0:T(8,128)}, u32[]{:S(2)}) copy-start(f32[32,30,16,128]{3,2,1,0:T(8,128)} %fields_ref.7) | copy-start | bytes 23592964
  96.6 17.5 %copy-start.3 = (f32[8,30,4,128]{3,2,1,0:T(4,128)S(1)}, f32[8,30,4,128]{3,2,1,0:T(4,128)}, u32[]{:S(2)}) copy-start(f32[8,30,4,128]{3,2,1,0:T(4,128)} %get-tuple-element.33) | copy-start | bytes 1474564
  114.1 39.5 %collective-permute-start.1 = (f32[8,30,4,128]{3,2,1,0:T(4,128)S(1)}, f32[8,30,4,128]{3,2,1,0:T(4,128)S(1)}, u32[]{:S(2)}, u32[]{:S(2)}) collective-permute-start(f32[8,30,4,128]{3,2,1,0:T(4,128)S(1)} %copy-done.3), channel_id=1, source_target_pairs={{0,8},{8,16},{16,24},{1,9},{9,17},{17,25},{2,10},{10,18},{18,26},{... | collective-permute-start | bytes 1474568 | tf_op jit(solution)/shard_map/ppermute | solution.py:340
  153.6 17.2 %copy-start.1 = (f32[32,16,128]{2,1,0:T(8,128)S(1)}, f32[32,16,128]{2,1,0:T(8,128)}, u32[]{:S(2)}) copy-start(f32[32,16,128]{2,1,0:T(8,128)} %param.15) | copy-start | bytes 786436
Sparse Core Ops, SparseCore 0:
  28.1 37.3 all-gather.2

commit v3 on v2

--- a/solution.py
+++ b/solution.py
@@ -9,7 +9,7 @@
 LEV = 10
 STEPS = 4
 SUB = 8
-CHUNKS = 4
+CHUNKS = 8
 EXT = 2 * STEPS
 F32 = jnp.float32
 BF16 = jnp.bfloat16
@@ -81,22 +81,86 @@
     out_ref[...] = x_ref[:, :, : out_ref.shape[2], :]
 
 
-def chunk_kernel(first, killed_ref, fields_ref, below_ref, above_ref, donor_ref, diff_ref, heat_ref, w_hi_ref, w_lo_ref, *rest):
-    out_ref, tq_ref, x_ref, y_hi_ref, y_lo_ref = rest[-5:]
-    steps_body(fields_ref, below_ref, above_ref, diff_ref, heat_ref, w_hi_ref, w_lo_ref, x_ref, y_hi_ref, y_lo_ref)
+def main_kernel(
+    fields_ref, low_ref, high_ref, diff_ref, heat_ref, w_hi_ref, w_lo_ref, out_ref, tq_ref,
+    below_ref, above_ref, x_ref, y_hi_ref, y_lo_ref, send_sem, recv_sem,
+):
     members, levels, own, lon = out_ref.shape
-    for g in range(members):
-        tq_ref[g, 0] = x_ref[g, 0, :own, :]
-        tq_ref[g, 1] = x_ref[g, LEV, :own, :]
-        killed = killed_ref[first + pl.program_id(0) * members + g] != 0
-
-        @pl.when(killed)
-        def _():
-            out_ref[g] = donor_ref[0]
-
-        @pl.when(jnp.logical_not(killed))
-        def _():
-            out_ref[g] = x_ref[g, :, :own, :]
+    group = x_ref.shape[0]
+    size = members // CHUNKS
+    me, bands = lax.axis_index("lat"), lax.axis_size("lat")
+
+    def halo(way, chunk, other):
+        part = pl.ds(chunk * size, size)
+        return pltpu.make_async_remote_copy(
+            src_ref=(low_ref, high_ref)[way].at[part],
+            dst_ref=(below_ref, above_ref)[way].at[part],
+            send_sem=send_sem.at[way, chunk],
+            recv_sem=recv_sem.at[way, chunk],
+            device_id={"lat": other},
+            device_id_type=pl.DeviceIdType.MESH,
+        )
+
+    greet(("lat",))
+
+    def begin(chunk, carry):
+        @pl.when(me > 0)
+        def _():
+            halo(0, chunk, me - 1).start()
+
+        @pl.when(me < bands - 1)
+        def _():
+            halo(1, chunk, me + 1).start()
+
+        return carry
+
+    lax.fori_loop(0, CHUNKS, begin, 0)
+
+    @pl.when(me == 0)
+    def _():
+        above_ref[...] = jnp.zeros_like(above_ref)
+
+    @pl.when(me == bands - 1)
+    def _():
+        below_ref[...] = jnp.zeros_like(below_ref)
+
+    def work(chunk, carry):
+        @pl.when(me > 0)
+        def _():
+            halo(1, chunk, me - 1).wait_recv()
+
+        @pl.when(me < bands - 1)
+        def _():
+            halo(0, chunk, me + 1).wait_recv()
+
+        def few(i, inner):
+            part = pl.ds(chunk * size + i * group, group)
+            steps_body(
+                fields_ref.at[part], below_ref.at[part], above_ref.at[part],
+                diff_ref, heat_ref, w_hi_ref, w_lo_ref, x_ref, y_hi_ref, y_lo_ref,
+            )
+            out_ref[part] = x_ref[:, :, :own, :]
+            tq_ref[part, 0] = x_ref[:, 0, :own, :]
+            tq_ref[part, 1] = x_ref[:, LEV, :own, :]
+            return inner
+
+        lax.fori_loop(0, size // group, few, 0)
+        return carry
+
+    lax.fori_loop(0, CHUNKS, work, 0)
+
+    def end(chunk, carry):
+        @pl.when(me > 0)
+        def _():
+            halo(0, chunk, me - 1).wait_send()
+
+        @pl.when(me < bands - 1)
+        def _():
+            halo(1, chunk, me + 1).wait_send()
+
+        return carry
+
+    lax.fori_loop(0, CHUNKS, end, 0)
 
 
 def peers(axis, send):
@@ -125,16 +189,16 @@
     peers(axis, lambda other, d: copy(other, me, d).wait_send())
 
 
-def greet():
+def greet(axes):
     barrier = pltpu.get_barrier_semaphore()
-    for axis in ("lat", "grp"):
+    for axis in axes:
         peers(
             axis,
             lambda other, d: pl.semaphore_signal(
                 barrier, inc=1, device_id={axis: other}, device_id_type=pl.DeviceIdType.MESH
             ),
         )
-    pl.semaphore_wait(barrier, lax.axis_size("lat") + lax.axis_size("grp") - 2)
+    pl.semaphore_wait(barrier, sum(lax.axis_size(axis) - 1 for axis in axes))
 
 
 def finish_kernel(
@@ -149,7 +213,7 @@
             at = 2 * m + k
             first_ref[at : at + 1, :] = tq_ref[m, k, 0:1, :]
             last_ref[at : at + 1, :] = tq_ref[m, k, own - 1 : own, :]
-    greet()
+    greet(("lat", "grp"))
 
     def edge(way, other):
         return pltpu.make_async_remote_copy(
@@ -269,36 +333,30 @@
     )(*ins)
 
 
-def run_chunk(index, size, killed, fields, below, above, donor, consts, held):
+def run_main(fields, consts):
     members, levels, own, lon = fields.shape
     group = 2
-    blocks = size // group
-    first = index * size
-    block = pl.BlockSpec((group, levels, own, lon), lambda i: (i + index * blocks, 0, 0, 0))
-    halo = pl.BlockSpec((group, levels, STEPS, lon), lambda i: (i, 0, 0, 0))
-    ins = [killed, fields, below, above, donor, *consts]
-    in_specs = [pl.BlockSpec(memory_space=pltpu.SMEM), block, halo, halo, full_spec(donor)]
-    in_specs += [full_spec(a) for a in consts]
-    alias = {}
-    if held is not None:
-        alias = {len(ins): 0}
-        ins.append(held)
-        in_specs.append(pl.BlockSpec(memory_space=pl.ANY))
-    flops = 6 * size * levels * levels * SUB * (own + EXT) * lon * STEPS
+    ins = (fields, fields[:, :, :STEPS], fields[:, :, own - STEPS :]) + consts
+    halo = pltpu.VMEM((members, levels, STEPS, lon), F32)
+    flops = 6 * members * levels * levels * SUB * (own + EXT) * lon * STEPS
     return pl.pallas_call(
-        functools.partial(chunk_kernel, first),
+        main_kernel,
         out_shape=(
             jax.ShapeDtypeStruct(fields.shape, F32),
-            jax.ShapeDtypeStruct((size, 2, own, lon), F32),
+            jax.ShapeDtypeStruct((members, 2, own, lon), F32),
         ),
-        in_specs=in_specs,
-        out_specs=(block, pl.BlockSpec((group, 2, own, lon), lambda i: (i, 0, 0, 0))),
-        grid=(blocks,),
-        scratch_shapes=steps_scratch(group, levels, own + EXT, lon),
-        input_output_aliases=alias,
-        compiler_params=params(),
-        cost_estimate=pl.CostEstimate(flops=flops, bytes_accessed=2 * size * levels * own * lon * 4, transcendentals=0),
-        name="chunk_steps",
+        in_specs=[pl.BlockSpec(memory_space=pltpu.VMEM)] * len(ins),
+        out_specs=(pl.BlockSpec(memory_space=pltpu.VMEM),) * 2,
+        scratch_shapes=[halo, halo]
+        + steps_scratch(group, levels, own + EXT, lon)
+        + [pltpu.SemaphoreType.DMA((2, CHUNKS)), pltpu.SemaphoreType.DMA((2, CHUNKS))],
+        compiler_params=pltpu.CompilerParams(
+            collective_id=1, has_side_effects=True, vmem_limit_bytes=56 * 2**20
+        ),
+        cost_estimate=pl.CostEstimate(
+            flops=10 * flops, bytes_accessed=3 * members * levels * own * lon * 4, transcendentals=0
+        ),
+        name="main_steps",
     )(*ins)
 
 
@@ -384,15 +442,8 @@
         donor_all[:, :, own + STEPS :],
         consts,
     )
-    size = members // CHUNKS
-    held, parts = None, []
-    for c in range(CHUNKS):
-        piece = lax.slice_in_dim(fields, c * size, (c + 1) * size, axis=0)
-        below, above = halos(piece, 2, STEPS)
-        held, tq = run_chunk(c, size, killed, fields, below, above, donor, consts, held)
-        parts.append(tq)
-    tq = jnp.concatenate(parts, axis=0)
-
+    final, tq = run_main(fields, consts)
+    new_fields = jnp.where(killed[:, None, None, None] > 0, donor, final)
     b_hi, b_lo = split_constant(conv_matrix(conv_weight, own))
     table = run_finish(tq, land_all, b_hi, b_lo, head_weight.reshape(-1, lon))
     all_scores = table[:, 0, :members].reshape(total_members)
@@ -402,7 +453,7 @@
     selector = (local_source[:, None] == jnp.arange(total_members, dtype=jnp.int32)[None, :]).astype(F32)
     chosen_weight = jnp.sum(selector * weights[None, :], 1)
     chosen_count = jnp.sum(selector * counts.astype(F32)[None, :], 1)
-    return held, scores, chosen_weight / chosen_count
+    return new_fields, scores, chosen_weight / chosen_count
 
 
 def solution(mesh):

time: 203 us -> 196 us (0.966)
  Pallas kernels: 93 us -> 127 us
  starting transfers between devices: 38.8 us -> 7.46 us
  waiting for transfers between devices: 16.1 us -> 0.02 us
  other arithmetic: 13.2 us -> 23.3 us
  local copies, waits for them, and re-layouts: 22 us -> 19.5 us
    pallas_call x4 -> x1, Pallas kernels: 68.8 us -> 99.3 us  [run_main(): pl.pallas_call(main_kernel, out_shape=(jax.ShapeDtypeStruct(fields.shape,...]
    ppermute x5 -> x1, starting transfers between devices: 32.4 us -> 6.14 us  [halos(): lax.ppermute(lax.slice_in_dim(value, length - width, length, axis=dim), a...]
    ppermute x5 -> x1, waiting for transfers between devices: 14.7 us -> 0.01 us  [halos(): lax.ppermute(lax.slice_in_dim(value, 0, width, axis=dim), axis, down)]
    select_n x0 -> x1, other arithmetic: none -> 7.23 us  [local(): new_fields = jnp.where(killed[:, None, None, None] > 0, donor, final)]
    ppermute x5 -> x1, starting transfers between devices: 6.44 us -> 1.28 us  [halos(): lax.ppermute(lax.slice_in_dim(value, 0, width, axis=dim), axis, down)]
    pallas_call x1, Pallas kernels: 21.6 us -> 24.7 us  [run_finish(): pl.pallas_call(finish_kernel, out_shape=jax.ShapeDtypeStruct((grp, SUB, l...]
    unnamed x19 -> x33, local copies, waits for them, and re-layouts: 3.98 us -> 1.18 us
    add x1, local copies, waits for them, and re-layouts: 4.07 us -> 1.92 us  [conv_matrix(): matrix = (parts[0] + parts[1] + parts[2]).reshape(channels * own, 9 * rows)]
  transfers between devices with their start and end apart: 11 -> 3, of which waited for: 3 -> 0; matrix products, arithmetic and copies ran while one was open for 12% -> 13% of each run, Pallas kernels for 27% -> 63%
where the time goes in v3:
time: 196 us
  Pallas kernels  127 us (65%)
  other arithmetic  23.3 us (12%)
  local copies, waits for them, and re-layouts  19.5 us (10%)
  between operations  18.9 us (10%)
  starting transfers between devices  7.46 us (4%)
    pallas_call x1, Pallas kernels, run_main(): pl.pallas_call(main_kernel, out_shape=(jax.ShapeDtypeStruct(fields.shape,...  99.3 us
    pallas_call x1, Pallas kernels, run_finish(): pl.pallas_call(finish_kernel, out_shape=jax.ShapeDtypeStruct((grp, SUB, l...  24.7 us
    select_n x1, other arithmetic, local(): new_fields = jnp.where(killed[:, None, None, None] > 0, donor, final)  7.23 us
    ppermute x1, starting transfers between devices, halos(): lax.ppermute(lax.slice_in_dim(value, length - width, length, axis=dim), a...  6.14 us
    slice x1, local copies, waits for them, and re-layouts, run_main(): ins = (fields, fields[:, :, :STEPS], fields[:, :, own - STEPS:]) + consts  5.94 us
  transfers between devices with their start and end apart: 3, of which 0 were waited for; matrix products, arithmetic and copies ran while one was open for 13% of the time, Pallas kernels for 63%

profile of v3, /device:TPU:0, one launch (start us, length us, event | category | flops | bytes accessed | tf_op | source)
XLA Modules:
  0.0 195.7 jit_solution(16907452783908135925)
XLA Ops:
  7.2 1.4 iota_reduce_fusion
  11.3 1.0 dynamic-slice_bitcast_fusion
  12.2 1.7 pad_maximum_fusion.4
  14.0 1.3 collective-permute-start
  15.3 6.1 %collective-permute-start.1 = (f32[62,4,128]{2,1,0:T(4,128)}, f32[62,4,128]{2,1,0:T(4,128)}, u32[]{:S(2)}, u32[]{:S(2)}) collective-permute-start(f32[62,4,128]{2,1,0:T(4,128)} %get-tuple-element.26), channel_id=1, source_target_pairs={{0,8},{8,16},{16,24},{1,9},{9,17},{17,25},{2,10},{10,18},{18,26},{... | collective-permute-start | bytes 380936 | tf_op jit(solution)/shard_map/ppermute | solution.py:398
  21.4 5.9 %fusion.8 = (f32[32,30,4,128]{3,2,1,0:T(4,128)}, f32[32,30,4,128]{3,2,1,0:T(4,128)}) fusion(f32[32,30,16,128]{3,2,1,0:T(8,128)} %fields_ref.1), kind=kLoop, calls=%fused_computation.50 | loop fusion | bytes 7864320 | tf_op jit(solution)/shard_map/slice | solution.py:339
  27.4 2.5 %broadcast_multiply_fusion = f32[30,8,30,8]{3,2,1,0:T(8,128)} fusion(f32[8,8]{1,0:T(8,128)S(1)} %fusion.3, f32[30,30]{1,0:T(8,128)S(1)} %copy-done.8), kind=kLoop, calls=%fused_computation.2 | loop fusion | flops 57600 | bytes 234256 | tf_op jit(solution)/shard_map/mul | solution.py:436
  29.9 3.7 %mul.97 = f32[240,240]{1,0:T(8,128)S(1)} reshape(f32[30,8,30,8]{3,2,1,0:T(8,128)} %broadcast_multiply_fusion) | data formatting | bytes 460800 | tf_op jit(solution)/shard_map/mul | solution.py:436
  34.5 0.7 copy.21
  35.2 0.7 copy.22
  35.9 0.7 copy.23
  37.4 2.2 %multiply_add_fusion = f32[32,16,3,3,24]{4,3,2,1,0:T(4,128)S(1)} fusion(f32[16,24]{1,0:T(8,128)S(1)} %get-tuple-element.30, f32[32,3,3]{2,1,0:T(4,128)} %copy.23, f32[16,24]{1,0:T(8,128)S(1)} %get-tuple-element.31, f32[32,3,3]{2,1,0:T(4,128)} %copy.22, f32[16,24]{1,0:T(8,128)S(1)} %get-tuple-element.29, f32[32,3,3]{2,1,0:T(4,128)} %copy.21), kind=kLoop, calls=%fused_computation.1 | loop fusion | flops 552960 | bytes 450432 | tf_op jit(solution)/shard_map/add | solution.py:412
  40.9 1.9 add.96
  44.8 1.1 fusion
  45.9 1.1 pad_maximum_fusion
  47.0 0.9 fusion.9
  48.0 1.3 maximum_bitcast_fusion
  49.3 99.3 %main_steps.1 = (f32[32,30,16,128]{3,2,1,0:T(8,128)}, f32[32,2,16,128]{3,2,1,0:T(8,128)}) custom-call(f32[32,30,16,128]{3,2,1,0:T(8,128)} %fields_ref.1, f32[32,30,4,128]{3,2,1,0:T(4,128)} %get-tuple-element.16.low_ref, f32[32,30,4,128]{3,2,1,0:T(4,128)} %get-tuple-element.15.high_ref, f32[24,128]{1,0:T(8,128)} %get-tuple-element.20.diff_ref, ...), custom_call_target="tpu_custom_call" | custom-call | flops 169869312000 | bytes 23592960 | tf_op jit(solution)/shard_map/main_steps/pallas_call | solution.py:342
  148.6 1.0 copy-done.1
  149.7 24.7 %finish.1 = f32[8,8,128]{2,1,0:T(8,128)S(1)} custom-call(f32[32,2,16,128]{3,2,1,0:T(8,128)S(1)} %copy-done.1, f32[24,128]{1,0:T(8,128)S(1)} %get-tuple-element.19.land_ref, bf16[512,224]{1,0:T(8,128)(2,1)S(1)} %get-tuple-element.24.b_hi_ref, bf16[512,224]{1,0:T(8,128)(2,1)S(1)} %get-tuple-element.23.b_lo_ref, f32[512,128]{1,0:T(8,128)S(1)} %bitcast.27), custom_call_target="tpu_custom_call" | custom-call | tf_op jit(solution)/shard_map/finish/pallas_call | solution.py:368
  177.1 1.0 constant_dynamic-slice_fusion.1.fields_ref
  178.0 1.0 constant_dynamic-slice_fusion.2
  179.1 2.5 %donor_steps.1 = f32[1,30,16,128]{3,2,1,0:T(8,128)S(1)} custom-call(f32[1,30,16,128]{3,2,1,0:T(8,128)S(1)} %constant_dynamic-slice_fusion.1.fields_ref, f32[1,30,4,128]{3,2,1,0:T(4,128)S(1)} %get-tuple-element.18.below_ref, f32[1,30,4,128]{3,2,1,0:T(4,128)S(1)} %get-tuple-element.17.above_ref, f32[24,128]{1,0:T(8,128)S(1)} %copy-done.5, ...), custom_call_target="tpu_custom_call" | custom-call | tf_op jit(solution)/shard_map/donor_steps/pallas_call | solution.py:324
  181.6 7.2 %broadcast_select_fusion = f32[32,30,16,128]{3,2,1,0:T(8,128)} fusion(f32[32,30,16,128]{3,2,1,0:T(8,128)} %get-tuple-element.7, f32[30,16,128]{2,1,0:T(8,128)S(1)} %bitcast.26, pred[32]{0:T(512)(128)(4,1)S(1)} %copy-done.12), kind=kLoop, calls=%fused_computation | loop fusion | flops 1966080 | bytes 15974432 | tf_op jit(solution)/shard_map/jit(_where)/select_n | solution.py:446
  (54 shorter events, 5.7 us)
Async XLA Ops:
  7.2 169.9 %all-gather.3.cloned.1.call-start = ((), (), s32[]{:S(2)}) async-start(), calls=%async_computation | async-start | bytes 3317760 | tf_op jit(solution)/shard_map/all_gather | solution.py:433
  14.0 31.9 %collective-permute-start = (f32[62,4,128]{2,1,0:T(4,128)}, f32[62,4,128]{2,1,0:T(4,128)S(1)}, u32[]{:S(2)}, u32[]{:S(2)}) collective-permute-start(f32[62,4,128]{2,1,0:T(4,128)} %get-tuple-element.25), channel_id=1, source_target_pairs={{8,0},{16,8},{24,16},{9,1},{17,9},{25,17},{10,2},{18,10},{26,18},{... | collective-permute-start | bytes 380936 | tf_op jit(solution)/shard_map/ppermute | solution.py:399
  15.3 30.6 %collective-permute-start.1 = (f32[62,4,128]{2,1,0:T(4,128)}, f32[62,4,128]{2,1,0:T(4,128)}, u32[]{:S(2)}, u32[]{:S(2)}) collective-permute-start(f32[62,4,128]{2,1,0:T(4,128)} %get-tuple-element.26), channel_id=1, source_target_pairs={{0,8},{8,16},{16,24},{1,9},{9,17},{17,25},{2,10},{10,18},{18,26},{... | collective-permute-start | bytes 380936 | tf_op jit(solution)/shard_map/ppermute | solution.py:398
  21.4 6.0 %copy-start.8 = (f32[30,30]{1,0:T(8,128)S(1)}, f32[30,30]{1,0:T(8,128)}, u32[]{:S(2)}) copy-start(f32[30,30]{1,0:T(8,128)} %param.11) | copy-start | bytes 10804
  29.9 4.5 %copy-start.9 = (f32[32,27]{1,0:T(8,128)S(1)}, f32[32,27]{1,0:T(8,128)}, u32[]{:S(2)}) copy-start(f32[32,27]{1,0:T(8,128)} %param.14) | copy-start | bytes 10372
  29.9 6.9 %copy-start.15 = (s32[256]{0:T(256)S(1)}, s32[256]{0:T(256)}, u32[]{:S(2)}) copy-start(s32[256]{0:T(256)} %param.17) | copy-start | bytes 3076
  33.6 6.7 %copy-start.11 = (s32[256]{0:T(256)S(1)}, s32[256]{0:T(256)}, u32[]{:S(2)}) copy-start(s32[256]{0:T(256)} %param.16) | copy-start | bytes 3076
  37.4 2.2 %copy-start.13 = (s32[32]{0:T(128)}, s32[32]{0:T(128)S(1)}, u32[]{:S(2)}) copy-start(s32[32]{0:T(128)S(1)} %get-tuple-element.14) | copy-start | bytes 388
  39.6 6.3 %copy-start.7 = (f32[16,128]{1,0:T(8,128)S(1)}, f32[16,128]{1,0:T(8,128)}, u32[]{:S(2)}) copy-start(f32[16,128]{1,0:T(8,128)} %param.10) | copy-start | bytes 24580
  42.8 5.2 %copy-start.6 = (f32[30,16,128]{2,1,0:T(8,128)S(1)}, f32[30,16,128]{2,1,0:T(8,128)}, u32[]{:S(2)}) copy-start(f32[30,16,128]{2,1,0:T(8,128)} %param.12) | copy-start | bytes 737284
  49.2 99.4 %copy-start.4 = (f32[32,16,128]{2,1,0:T(8,128)S(1)}, f32[32,16,128]{2,1,0:T(8,128)}, u32[]{:S(2)}) copy-start(f32[32,16,128]{2,1,0:T(8,128)} %param.15) | copy-start | bytes 786436
  49.2 127.1 %copy-start.10 = (f32[256]{0:T(256)S(1)}, f32[256]{0:T(256)}, u32[]{:S(2)}) copy-start(f32[256]{0:T(256)} %convert_element_type.46) | copy-start | bytes 3076
  49.3 127.1 %copy-start.14 = (s32[32]{0:T(128)S(1)}, s32[32]{0:T(128)}, u32[]{:S(2)}) copy-start(s32[32]{0:T(128)} %copy-done.13) | copy-start | bytes 388
  49.3 129.8 %copy-start = (f32[30,24,128]{2,1,0:T(8,128)S(1)}, f32[30,24,128]{2,1,0:T(8,128)}, u32[]{:S(2)}) copy-start(f32[30,24,128]{2,1,0:T(8,128)} %get-tuple-element.22.heat_ref) | copy-start | bytes 1105924
  49.3 129.8 %copy-start.2 = (bf16[240,240]{1,0:T(8,128)(2,1)S(1)}, bf16[240,240]{1,0:T(8,128)(2,1)}, u32[]{:S(2)}) copy-start(bf16[240,240]{1,0:T(8,128)(2,1)} %get-tuple-element.27.w_lo_ref) | copy-start | bytes 345604
  49.3 129.8 %copy-start.3 = (bf16[240,240]{1,0:T(8,128)(2,1)S(1)}, bf16[240,240]{1,0:T(8,128)(2,1)}, u32[]{:S(2)}) copy-start(bf16[240,240]{1,0:T(8,128)(2,1)} %get-tuple-element.28.w_hi_ref) | copy-start | bytes 345604
  49.3 129.8 %copy-start.5 = (f32[24,128]{1,0:T(8,128)S(1)}, f32[24,128]{1,0:T(8,128)}, u32[]{:S(2)}) copy-start(f32[24,128]{1,0:T(8,128)} %get-tuple-element.20.diff_ref) | copy-start | bytes 36868
  148.6 33.0 %copy-start.12 = (pred[32]{0:T(512)(128)(4,1)S(1)}, pred[32]{0:T(512)(128)(4,1)}, u32[]{:S(2)}) copy-start(pred[32]{0:T(512)(128)(4,1)} %get-tuple-element.13) | copy-start | bytes 100
  148.6 1.0 copy-start.1
Sparse Core Ops, SparseCore 0:
  48.1 37.7 all-gather.2

commit v4 on v3

--- a/solution.py
+++ b/solution.py
@@ -400,18 +400,30 @@
     return below, above
 
 
+def spread(value, width, run):
+    col = lax.broadcasted_iota(jnp.int32, (value.shape[1], width), 1)
+    row = lax.broadcasted_iota(jnp.int32, (value.shape[1], width), 0)
+    return jnp.dot(value, (col // run == row).astype(F32), precision=lax.Precision.HIGHEST)
+
+
 def conv_matrix(conv_weight, own):
     rows = own + SUB
     channels = conv_weight.shape[0]
-    taps = conv_weight.reshape(channels, 1, 3, 3, 3, 1)
-    i = jnp.arange(own)[:, None, None]
-    a = jnp.arange(3)[None, :, None]
-    r = jnp.arange(rows)[None, None, :]
-    hit = ((i + a - 1) % rows == r).astype(F32)
-    parts = [taps[:, :, :, k] * hit[None, :, None, None, k, :] for k in range(3)]
-    matrix = (parts[0] + parts[1] + parts[2]).reshape(channels * own, 9 * rows)
-    pad = -matrix.shape[1] % 16
-    return jnp.pad(matrix, ((0, 0), (0, pad)))
+    width = 9 * rows + (-9 * rows) % 16
+    taps = conv_weight.reshape(channels, 3, 3, 3).transpose(2, 0, 1, 3).reshape(3 * channels, 9)
+    taps = spread(taps, width, rows).reshape(3, channels, 1, width)
+    i = lax.broadcasted_iota(jnp.int32, (1, own, width), 1)
+    r = lax.broadcasted_iota(jnp.int32, (1, own, width), 2) % rows
+    parts = [jnp.where((i + a - 1 + rows) % rows == r, taps[a], 0.0) for a in range(3)]
+    return (parts[0] + parts[1] + parts[2]).reshape(channels * own, width)
+
+
+def mixing_matrix(mixing):
+    levels = mixing.shape[0]
+    i = lax.broadcasted_iota(jnp.int32, (1, SUB, levels * SUB), 1)
+    r = lax.broadcasted_iota(jnp.int32, (1, SUB, levels * SUB), 2) % SUB
+    wide = jnp.where(i == r, spread(mixing, levels * SUB, SUB)[:, None, :], 0.0)
+    return wide.reshape(levels * SUB, levels * SUB)
 
 
 def local(fields, diffusion, mixing, heating, land_mask, conv_weight, head_weight, counts, source):
@@ -432,9 +444,7 @@
     diff_all, land_all = stack_all[2 * levels], stack_all[2 * levels + 1]
     gathered = lax.all_gather(hot_all, "grp", axis=0)
     donor_all = lax.dynamic_index_in_dim(gathered, donor_group, 0, keepdims=True)
-    eye = jnp.eye(SUB, dtype=F32)
-    wide = (mixing[:, None, :, None] * eye[None, :, None, :]).reshape(levels * SUB, levels * SUB)
-    consts = (diff_all, heat_all, *split_constant(wide))
+    consts = (diff_all, heat_all, *split_constant(mixing_matrix(mixing)))
 
     donor = run_donor(
         donor_all[:, :, :own],

time: 196 us -> 181 us (0.923)
  other arithmetic: 23.3 us -> 15.3 us
  local copies, waits for them, and re-layouts: 19.5 us -> 12.3 us
    mul x6 -> x0, local copies, waits for them, and re-layouts: 5.93 us -> none  [the longest x1 3.71 us: local(): mixing[:, None, :, None] * eye[None, :, None, :]]
    mul x1 -> x0, other arithmetic: 2.49 us -> none  [local(): mixing[:, None, :, None] * eye[None, :, None, :]]
    add x1 -> x2, other arithmetic: 2.19 us -> 0.13 us  [the longest x1 0.12 us: conv_matrix(): return (parts[0] + parts[1] + parts[2]).reshape(channels * own, width)]
  transfers between devices with their start and end apart: 3 -> 3, of which waited for: 0 -> 0; matrix products, arithmetic and copies ran while one was open for 13% -> 7% of each run, Pallas kernels for 63% -> 69%
where the time goes in v4:
time: 181 us
  Pallas kernels  127 us (70%)
  between operations  18.9 us (10%)
  other arithmetic  15.3 us (8%)
  local copies, waits for them, and re-layouts  12.3 us (7%)
  starting transfers between devices  6.81 us (4%)
    pallas_call x1, Pallas kernels, run_main(): pl.pallas_call(main_kernel, out_shape=(jax.ShapeDtypeStruct(fields.shape,...  100 us
    pallas_call x1, Pallas kernels, run_finish(): pl.pallas_call(finish_kernel, out_shape=jax.ShapeDtypeStruct((grp, SUB, l...  24.7 us
    select_n x1, other arithmetic, local(): new_fields = jnp.where(killed[:, None, None, None] > 0, donor, final)  7.21 us
    slice x1, local copies, waits for them, and re-layouts, run_main(): ins = (fields, fields[:, :, :STEPS], fields[:, :, own - STEPS:]) + consts  5.91 us
    ppermute x1, starting transfers between devices, halos(): lax.ppermute(lax.slice_in_dim(value, length - width, length, axis=dim), a...  5.48 us
  transfers between devices with their start and end apart: 3, of which 0 were waited for; matrix products, arithmetic and copies ran while one was open for 7% of the time, Pallas kernels for 69%

profile of v4, /device:TPU:0, one launch (start us, length us, event | category | flops | bytes accessed | tf_op | source)
XLA Modules:
  0.0 180.9 jit_solution(18152052712256606602)
XLA Ops:
  7.3 1.4 iota_reduce_fusion
  10.0 0.7 convert_bitcast_fusion
  11.4 1.0 dynamic-slice_bitcast_fusion
  12.3 1.0 pad_maximum_fusion.4
  13.4 1.3 collective-permute-start
  14.7 5.5 %collective-permute-start.1 = (f32[62,4,128]{2,1,0:T(4,128)S(1)}, f32[62,4,128]{2,1,0:T(4,128)S(1)}, u32[]{:S(2)}, u32[]{:S(2)}) collective-permute-start(f32[62,4,128]{2,1,0:T(4,128)S(1)} %get-tuple-element.26), channel_id=1, source_target_pairs={{0,8},{8,16},{16,24},{1,9},{9,17},{17,25},{2,10},{10,18},{18,26},{... | collective-permute-start | bytes 380936 | tf_op jit(solution)/shard_map/ppermute | solution.py:398
  20.2 5.9 %fusion.13 = (f32[32,30,4,128]{3,2,1,0:T(4,128)}, f32[32,30,4,128]{3,2,1,0:T(4,128)}) fusion(f32[32,30,16,128]{3,2,1,0:T(8,128)} %fields_ref.1), kind=kLoop, calls=%fused_computation.70 | loop fusion | bytes 7864320 | tf_op jit(solution)/shard_map/slice | solution.py:339
  26.2 0.6 convert_element_type.30
  27.6 0.6 fusion.12
  28.2 0.5 copy-done.13
  28.7 0.6 select_reduce_fusion.2
  31.4 0.7 fusion.1
  32.3 0.9 fusion.14
  33.2 0.6 maximum_bitcast_fusion
  33.9 100.0 %main_steps.1 = (f32[32,30,16,128]{3,2,1,0:T(8,128)}, f32[32,2,16,128]{3,2,1,0:T(8,128)}) custom-call(f32[32,30,16,128]{3,2,1,0:T(8,128)} %fields_ref.1, f32[32,30,4,128]{3,2,1,0:T(4,128)} %get-tuple-element.16.low_ref, f32[32,30,4,128]{3,2,1,0:T(4,128)} %get-tuple-element.15.high_ref, f32[24,128]{1,0:T(8,128)} %get-tuple-element.20.diff_ref, ...), custom_call_target="tpu_custom_call" | custom-call | flops 169869312000 | bytes 23592960 | tf_op jit(solution)/shard_map/main_steps/pallas_call | solution.py:342
  133.9 1.0 copy-done.2
  134.9 24.7 %finish.1 = f32[8,8,128]{2,1,0:T(8,128)S(1)} custom-call(f32[32,2,16,128]{3,2,1,0:T(8,128)S(1)} %copy-done.2, f32[24,128]{1,0:T(8,128)S(1)} %get-tuple-element.19.land_ref, bf16[512,224]{1,0:T(8,128)(2,1)S(1)} %get-tuple-element.24.b_hi_ref, bf16[512,224]{1,0:T(8,128)(2,1)S(1)} %get-tuple-element.23.b_lo_ref, f32[512,128]{1,0:T(8,128)S(1)} %bitcast.30), custom_call_target="tpu_custom_call" | custom-call | tf_op jit(solution)/shard_map/finish/pallas_call | solution.py:368
  159.6 0.6 exponential_reduce_fusion
  160.3 0.6 dynamic_slice.21
  161.8 0.5 div.54
  162.3 1.0 constant_dynamic-slice_fusion.1.fields_ref
  163.3 1.0 constant_dynamic-slice_fusion.2
  164.3 2.5 %donor_steps.1 = f32[1,30,16,128]{3,2,1,0:T(8,128)S(1)} custom-call(f32[1,30,16,128]{3,2,1,0:T(8,128)S(1)} %constant_dynamic-slice_fusion.1.fields_ref, f32[1,30,4,128]{3,2,1,0:T(4,128)S(1)} %get-tuple-element.18.below_ref, f32[1,30,4,128]{3,2,1,0:T(4,128)S(1)} %get-tuple-element.17.above_ref, f32[24,128]{1,0:T(8,128)S(1)} %copy-done.6, ...), custom_call_target="tpu_custom_call" | custom-call | tf_op jit(solution)/shard_map/donor_steps/pallas_call | solution.py:324
  166.9 7.2 %broadcast_select_fusion = f32[32,30,16,128]{3,2,1,0:T(8,128)} fusion(f32[32,30,16,128]{3,2,1,0:T(8,128)} %get-tuple-element.7, f32[30,16,128]{2,1,0:T(8,128)S(1)} %bitcast.29, pred[32]{0:T(512)(128)(4,1)S(1)} %copy-done.12), kind=kLoop, calls=%fused_computation | loop fusion | flops 1966080 | bytes 15974432 | tf_op jit(solution)/shard_map/jit(_where)/select_n | solution.py:456
  (59 shorter events, 1.4 us)
Async XLA Ops:
  7.2 24.1 %copy-start = (f32[30,30]{1,0:T(8,128)S(1)}, f32[30,30]{1,0:T(8,128)}, u32[]{:S(2)}) copy-start(f32[30,30]{1,0:T(8,128)} %param.11) | copy-start | bytes 10804
  7.2 19.0 %copy-start.11 = (s32[256]{0:T(256)S(1)}, s32[256]{0:T(256)}, u32[]{:S(2)}) copy-start(s32[256]{0:T(256)} %param.16) | copy-start | bytes 3076
  7.2 25.0 %copy-start.8 = (f32[16,128]{1,0:T(8,128)S(1)}, f32[16,128]{1,0:T(8,128)}, u32[]{:S(2)}) copy-start(f32[16,128]{1,0:T(8,128)} %param.10) | copy-start | bytes 24580
  7.2 25.0 %copy-start.7 = (f32[30,16,128]{2,1,0:T(8,128)S(1)}, f32[30,16,128]{2,1,0:T(8,128)}, u32[]{:S(2)}) copy-start(f32[30,16,128]{2,1,0:T(8,128)} %param.12) | copy-start | bytes 737284
  7.2 19.6 %copy-start.9 = (f32[32,27]{1,0:T(8,128)S(1)}, f32[32,27]{1,0:T(8,128)}, u32[]{:S(2)}) copy-start(f32[32,27]{1,0:T(8,128)} %param.14) | copy-start | bytes 10372
  7.2 20.3 %copy-start.15 = (s32[256]{0:T(256)S(1)}, s32[256]{0:T(256)}, u32[]{:S(2)}) copy-start(s32[256]{0:T(256)} %param.17) | copy-start | bytes 3076
  7.2 155.1 %all-gather.3.cloned.1.call-start = ((), (), s32[]{:S(2)}) async-start(), calls=%async_computation | async-start | bytes 3317760 | tf_op jit(solution)/shard_map/all_gather | solution.py:445
  13.4 18.8 %collective-permute-start = (f32[62,4,128]{2,1,0:T(4,128)S(1)}, f32[62,4,128]{2,1,0:T(4,128)S(1)}, u32[]{:S(2)}, u32[]{:S(2)}) collective-permute-start(f32[62,4,128]{2,1,0:T(4,128)S(1)} %get-tuple-element.25), channel_id=1, source_target_pairs={{8,0},{16,8},{24,16},{9,1},{17,9},{25,17},{10,2},{18,10},{26,18},{... | collective-permute-start | bytes 380936 | tf_op jit(solution)/shard_map/ppermute | solution.py:399
  14.7 17.5 %collective-permute-start.1 = (f32[62,4,128]{2,1,0:T(4,128)S(1)}, f32[62,4,128]{2,1,0:T(4,128)S(1)}, u32[]{:S(2)}, u32[]{:S(2)}) collective-permute-start(f32[62,4,128]{2,1,0:T(4,128)S(1)} %get-tuple-element.26), channel_id=1, source_target_pairs={{0,8},{8,16},{16,24},{1,9},{9,17},{17,25},{2,10},{10,18},{18,26},{... | collective-permute-start | bytes 380936 | tf_op jit(solution)/shard_map/ppermute | solution.py:398
  28.2 0.5 copy-start.13
  33.9 100.0 %copy-start.5 = (f32[32,16,128]{2,1,0:T(8,128)S(1)}, f32[32,16,128]{2,1,0:T(8,128)}, u32[]{:S(2)}) copy-start(f32[32,16,128]{2,1,0:T(8,128)} %param.15) | copy-start | bytes 786436
  33.9 127.7 %copy-start.10 = (f32[256]{0:T(256)S(1)}, f32[256]{0:T(256)}, u32[]{:S(2)}) copy-start(f32[256]{0:T(256)} %convert_element_type.30) | copy-start | bytes 3076
  33.9 127.7 %copy-start.14 = (s32[32]{0:T(128)S(1)}, s32[32]{0:T(128)}, u32[]{:S(2)}) copy-start(s32[32]{0:T(128)} %copy-done.13) | copy-start | bytes 388
  33.9 130.4 %copy-start.1 = (f32[30,24,128]{2,1,0:T(8,128)S(1)}, f32[30,24,128]{2,1,0:T(8,128)}, u32[]{:S(2)}) copy-start(f32[30,24,128]{2,1,0:T(8,128)} %get-tuple-element.22.heat_ref) | copy-start | bytes 1105924
  33.9 130.4 %copy-start.3 = (bf16[240,240]{1,0:T(8,128)(2,1)S(1)}, bf16[240,240]{1,0:T(8,128)(2,1)}, u32[]{:S(2)}) copy-start(bf16[240,240]{1,0:T(8,128)(2,1)} %get-tuple-element.30.w_lo_ref) | copy-start | bytes 345604
  33.9 130.4 %copy-start.4 = (bf16[240,240]{1,0:T(8,128)(2,1)S(1)}, bf16[240,240]{1,0:T(8,128)(2,1)}, u32[]{:S(2)}) copy-start(bf16[240,240]{1,0:T(8,128)(2,1)} %get-tuple-element.31.w_hi_ref) | copy-start | bytes 345604
  33.9 130.4 %copy-start.6 = (f32[24,128]{1,0:T(8,128)S(1)}, f32[24,128]{1,0:T(8,128)}, u32[]{:S(2)}) copy-start(f32[24,128]{1,0:T(8,128)} %get-tuple-element.20.diff_ref) | copy-start | bytes 36868
  33.9 133.0 %copy-start.12 = (pred[32]{0:T(512)(128)(4,1)S(1)}, pred[32]{0:T(512)(128)(4,1)}, u32[]{:S(2)}) copy-start(pred[32]{0:T(512)(128)(4,1)} %get-tuple-element.13) | copy-start | bytes 100
  133.9 1.0 copy-start.2
Sparse Core Ops, SparseCore 0:
  33.4 38.3 all-gather.2
